TPU v7x, 32 devices: a whole 2x2x4 slice. The times are simulated.
32 devices in a mesh: groups: 2 (over x), seq: 8 (over z, y), mp: 2 (over core).
Axes of the slice: x: 2, y: 2, z: 4, core: 2. Of those that a mesh axis runs over, the one named last changes fastest.
Arguments:
- inputs: bfloat16 [8192, 2560], P(('groups', 'seq')), parts along dimension 0, may hold values from -6 to 6
- zx_weight: bfloat16 [2560, 2, 2560], P('seq', None, 'mp'), may hold values from -0.125 to 0.125
- bc_weight: bfloat16 [2560, 256], P('seq'), may hold values from -0.125 to 0.125
- dt_weight: bfloat16 [2560, 40], P('seq', 'mp'), may hold values from -0.125 to 0.125
- conv_x: float32 [4, 2560], P(None, 'mp'), may hold values from -3 to 3
- conv_x_bias: float32 [2560], P('mp'), may hold values from -3 to 3
- conv_bc: float32 [4, 256], replicated, may hold values from -3 to 3
- conv_bc_bias: float32 [256], replicated, may hold values from -3 to 3
- dt_bias: float32 [40], P('mp'), may hold values from -4 to -3
- decay_log: float32 [40], P('mp'), may hold values from -9 to 0.5
- skip_gain: float32 [40], P('mp'), may hold values from 0.5 to 1.5
- norm_gain: float32 [2560], P('mp'), may hold values from 0.1 to 1.9
- out_weight: bfloat16 [2560, 2560], P('mp', 'seq'), may hold values from -0.125 to 0.125
Outputs:
- mixed: bfloat16 [8192, 2560], P(('groups', 'seq'), 'mp'), parts along dimension 0
There are 2 independent parts, one for each index of `groups`. A program takes and returns all parts, laid end to end along the dimension named above; an argument that names none is the same for every part. Nothing has to cross between parts.
All inputs are finite; a program needn't handle non-finite values.
Results may differ from a plain program's by a relative error of at most 0.0063.
Values may be sent and summed in bfloat16 or wider, within the bound.
A program may use at most 128 MiB of HBM per device.

v0:
```python
import jax
import jax.numpy as jnp
from jax import lax
from jax.sharding import PartitionSpec as P

STRETCH = 256


HIGHEST = lax.Precision.HIGHEST
NORM_EPS = 1e-05


def shifted(block, axis, distance):
    devices = range(lax.axis_size(axis))
    route = [(i - distance, i) for i in devices if i - distance in devices]
    return lax.ppermute(block, axis, route)


def conv_silu(padded, kernel, bias_row):
    taps = kernel.shape[0]
    length = padded.shape[0] - taps + 1
    total = jnp.zeros((length, padded.shape[1]), jnp.float32) + bias_row[None, :]
    for tap_index in range(taps):
        total = total + kernel[tap_index][None, :] * padded[tap_index : tap_index + length]
    return jax.nn.silu(total).astype(jnp.bfloat16)


def block_step(state_in, block_inputs):
    values, steps_dt, log_decay, keys_b, queries_c = block_inputs
    span = log_decay.shape[0]
    cumulative = jnp.cumsum(log_decay, axis=0)
    positions = jnp.arange(span)
    causal = positions[:, None] >= positions[None, :]
    across = cumulative.T[:, :, None] - cumulative.T[:, None, :]
    decays = jnp.exp(jnp.where(causal[None, :, :], across, -jnp.inf))
    scores = jnp.dot(queries_c, keys_b.T, preferred_element_type=jnp.float32)
    mixing = (decays * scores[None, :, :] * steps_dt.T[:, None, :]).astype(jnp.bfloat16)
    inner = jnp.einsum("hts,shp->thp", mixing, values, preferred_element_type=jnp.float32)
    queries_wide = queries_c.astype(jnp.float32)
    entering = (
        jnp.einsum("tn,hpn->thp", queries_wide, state_in, precision=HIGHEST)
        * jnp.exp(cumulative)[:, :, None]
    )
    tail_decay = jnp.exp(cumulative[-1][None, :] - cumulative) * steps_dt
    weighted = (tail_decay[:, :, None] * values.astype(jnp.float32)).astype(jnp.bfloat16)
    state_out = jnp.exp(cumulative[-1])[:, None, None] * state_in + jnp.einsum(
        "shp,sn->hpn", weighted, keys_b, preferred_element_type=jnp.float32
    )
    return (state_out, inner + entering)


def run_blocks(values, steps_dt, log_decay, keys_b, queries_c):
    length, head_count, head_dim = values.shape
    blocks = length // STRETCH
    state_dim = keys_b.shape[1]

    def to_blocks(array):
        return array.reshape((blocks, STRETCH) + array.shape[1:])

    start_state = jnp.zeros((head_count, head_dim, state_dim), jnp.float32)
    final_state, outputs = lax.scan(
        block_step,
        start_state,
        (
            to_blocks(values),
            to_blocks(steps_dt),
            to_blocks(log_decay),
            to_blocks(keys_b),
            to_blocks(queries_c),
        ),
    )
    return (final_state, outputs.reshape(length, head_count, head_dim))


def shards(
    inputs,
    zx_weight,
    bc_weight,
    dt_weight,
    conv_x,
    conv_x_bias,
    conv_bc,
    conv_bc_bias,
    dt_bias,
    decay_log,
    skip_gain,
    norm_gain,
    out_weight,
):
    row_count = inputs.shape[0]
    width_local = conv_x.shape[1]
    head_count = dt_weight.shape[1]
    head_dim = width_local // head_count
    state_dim = bc_weight.shape[1] // 2
    taps = conv_x.shape[0]
    pieces = (
        lax.all_gather(zx_weight, "seq", axis=0, tiled=True),
        lax.all_gather(bc_weight, "seq", axis=0, tiled=True),
        lax.all_gather(dt_weight, "seq", axis=0, tiled=True),
    )
    piece_rows = pieces[0].shape[0]
    zx_sum = jnp.dot(
        inputs, pieces[0].reshape(piece_rows, 2 * width_local), preferred_element_type=jnp.float32
    )
    bc_sum = jnp.dot(inputs, pieces[1], preferred_element_type=jnp.float32)
    dt_raw = jnp.dot(inputs, pieces[2], preferred_element_type=jnp.float32)
    projected = zx_sum.astype(jnp.bfloat16)
    gate_z = projected[:, :width_local]
    raw_x = projected[:, width_local:]
    raw_all = jnp.concatenate([raw_x, bc_sum.astype(jnp.bfloat16)], axis=1)
    rim_rows = shifted(raw_all[row_count - (taps - 1) :], "seq", 1)
    padded = jnp.concatenate([rim_rows, raw_all], axis=0).astype(jnp.float32)
    mixed_conv = conv_silu(
        padded,
        jnp.concatenate([conv_x, conv_bc], axis=1),
        jnp.concatenate([conv_x_bias, conv_bc_bias]),
    )
    values = mixed_conv[:, :width_local].reshape(row_count, head_count, head_dim)
    keys_b = mixed_conv[:, width_local : width_local + state_dim]
    queries_c = mixed_conv[:, width_local + state_dim :]
    steps_dt = jax.nn.softplus(dt_raw + dt_bias[None, :])
    log_decay = -jnp.exp(decay_log)[None, :] * steps_dt
    local_state, scanned = run_blocks(values, steps_dt, log_decay, keys_b, queries_c)
    cumulative = jnp.cumsum(log_decay, axis=0)
    shard_decay = jnp.exp(cumulative[-1])

    def pass_once(turn_index, carried):
        return shifted(shard_decay[:, None, None] * carried + local_state, "seq", 1)

    incoming = lax.fori_loop(0, lax.axis_size("seq") - 1, pass_once, jnp.zeros_like(local_state))
    entering = (
        jnp.einsum("tn,hpn->thp", queries_c.astype(jnp.float32), incoming, precision=HIGHEST)
        * jnp.exp(cumulative)[:, :, None]
    )
    output_y = scanned + entering + skip_gain[None, :, None] * values.astype(jnp.float32)
    gated = output_y.reshape(row_count, width_local) * jax.nn.silu(gate_z.astype(jnp.float32))
    total_square = lax.psum(jnp.sum(gated * gated, axis=1), "mp")
    mean_square = total_square / (width_local * lax.axis_size("mp"))
    normed = (gated * lax.rsqrt(mean_square + NORM_EPS)[:, None] * norm_gain[None, :]).astype(
        jnp.bfloat16
    )
    partial_out = jnp.dot(
        normed,
        lax.all_gather(out_weight, "seq", axis=1, tiled=True),
        preferred_element_type=jnp.float32,
    )
    return lax.psum_scatter(partial_out, "mp", scatter_dimension=1, tiled=True).astype(jnp.bfloat16)


def solution(mesh):
    return jax.shard_map(
        shards,
        mesh=mesh,
        in_specs=(
            P(("groups", "seq"), None),
            P("seq", None, "mp"),
            P("seq", None),
            P("seq", "mp"),
            P(None, "mp"),
            P("mp"),
            P(),
            P(),
            P("mp"),
            P("mp"),
            P("mp"),
            P("mp"),
            P("mp", "seq"),
        ),
        out_specs=P(("groups", "seq"), "mp"),
        check_vma=False,
    )
```

profile of v0, /device:TPU:29, one launch (start us, length us, event | category | flops | bytes accessed | tf_op | source)
XLA Modules:
  0.0 506.4 jit_solution(10535066734636534203)
XLA Ops:
  9.0 24.4 %all-gather = bf16[8,320,20]{1,2,0:T(8,128)(2,1)S(1)} all-gather(bf16[1,320,20]{1,2,0:T(8,128)(2,1)S(1)} %bitcast.135), channel_id=1, replica_groups=mesh['groups'=2,'seq'=8,'mp'=2] {'seq'}, dimensions={0}, use_global_device_ids=true | all-gather | bytes 115200 | tf_op jit(solution)/shard_map/all_gather | solution.py:99
  36.8 12.8 %all-gather.7.cloned.1.call-done = bf16[2560,256]{1,0:T(8,128)(2,1)} async-done(((bf16[320,256]{1,0:T(8,128)(2,1)}), bf16[2560,256]{1,0:T(8,128)(2,1)}) %all-gather.7.cloned.1.call-update) | async-done | bytes 1310736 | tf_op jit(solution)/shard_map/all_gather | solution.py:98
  49.6 2.2 convolution_convert_fusion.1
  51.8 181.9 %all-gather.5.cloned.1.call-done = bf16[2560,2,1280]{2,1,0:T(2,128)(2,1)} async-done(((bf16[320,2,1280]{2,1,0:T(2,128)(2,1)}), bf16[2560,2,1280]{2,1,0:T(2,128)(2,1)}) %all-gather.5.cloned.1.call-update) | async-done | bytes 13107216 | tf_op jit(solution)/shard_map/all_gather | solution.py:97
  233.7 8.3 %copy.75 = bf16[320,8,2,1280]{3,1,2,0:T(8,128)(2,1)S(1)} copy(bf16[320,8,2,1280]{3,2,1,0:T(2,128)(2,1)} %bitcast.120) | data formatting | bytes 26214400
  242.0 8.3 %convolution_convert_fusion = bf16[512,2560]{1,0:T(8,128)(2,1)} fusion(bf16[512,2560]{1,0:T(8,128)(2,1)S(1)} %copy-done, bf16[2560,2560]{1,0:T(8,128)(2,1)S(1)} %bitcast.121), kind=kOutput, calls=%fused_computation.49 | convolution fusion | flops 6712197120 | bytes 18350080 | tf_op jit(solution)/shard_map/dot_general | solution.py:102
  251.8 1.5 collective-permute-start.1
  254.6 2.0 collective-permute-done.1
  257.1 2.0 multiply_convert_fusion.5
  259.1 1.9 fusion.56
  263.4 71.0 %while.24 = (s32[]{:T(128)}, f32[20,64,128]{2,1,0:T(8,128)S(1)}, f32[2,256,20,64]{1,0,3,2:T(2,128)}, f32[2,256,20]{1,0,2:T(2,128)}, f32[2,256,20]{1,0,2:T(2,128)...) while((s32[]{:T(128)}, f32[20,64,128]{2,1,0:T(8,128)S(1)}, ...), condition=%wide.region_3.4_spmd.clone, body=%wide.region_0.3_spmd.clone.sunk | while | flops 781330496 | bytes 14201100 | solution.py:61
  265.5 1.5 fusion.83
  270.7 27.1 %dynamic_update_slice.6 = f32[2,256,20,64]{1,0,3,2:T(2,128)} dynamic-update-slice(f32[2,256,20,64]{1,0,3,2:T(2,128)} %get-tuple-element.266, f32[1,256,20,64]{1,0,3,2:T(1,128)S(1)} %copy.95, s32[]{:T(128)} %get-tuple-element.264, s32[]{:T(128)} %constant.41.clone.1..sunk, s32[]{:T(128)} %constant.41.clone.1..sunk, s32[]{:T(128)} %constant.41.clone.1..sunk) | dynamic-update-slice | bytes 2621444 | tf_op jit(solution)/shard_map/while/body/jit(dynamic_update_index_in_dim)/dynamic_update_slice | solution.py:61
  301.0 1.5 fusion.83
  306.2 27.1 %dynamic_update_slice.6 = f32[2,256,20,64]{1,0,3,2:T(2,128)} dynamic-update-slice(f32[2,256,20,64]{1,0,3,2:T(2,128)} %get-tuple-element.266, f32[1,256,20,64]{1,0,3,2:T(1,128)S(1)} %copy.95, s32[]{:T(128)} %get-tuple-element.264, s32[]{:T(128)} %constant.41.clone.1..sunk, s32[]{:T(128)} %constant.41.clone.1..sunk, s32[]{:T(128)} %constant.41.clone.1..sunk) | dynamic-update-slice | bytes 2621444 | tf_op jit(solution)/shard_map/while/body/jit(dynamic_update_index_in_dim)/dynamic_update_slice | solution.py:61
  334.4 4.9 reshape.102
  339.3 2.1 copy.64
  341.5 110.8 %while.23 = (s32[]{:T(128)}, f32[20,64,128]{2,1,0:T(8,128)S(1)}, f32[20]{0:T(128)S(1)}, f32[20,64,128]{2,1,0:T(8,128)S(1)}, s32[]{:T(128)}) while((s32[]{:T(128)}, f32[20,64,128]{2,1,0:T(8,128)S(1)}, f32[20]{0:T(128)S(1)}, f32[20,64,128]{2,1,0:T(8,128)S(1)}, s32[]{:T(128)}) %tuple.55), condition=%wide.region_7.8_spmd, body=%wide.region_6.7_spmd.sunk | while | flops 327682 | bytes 4587701 | solution.py:130
  343.0 18.2 %collective-permute-done = f32[20,64,128]{2,1,0:T(8,128)S(1)} collective-permute-done((f32[20,64,128]{2,1,0:T(8,128)S(1)}, f32[20,64,128]{2,1,0:T(8,128)S(1)}, u32[]{:S(2)}, u32[]{:S(2)}) %collective-permute-start) | collective-permute-done | bytes 655392 | tf_op jit(solution)/shard_map/while/body/eval_jaxpr/ppermute | solution.py:16
  362.6 16.0 %collective-permute-done = f32[20,64,128]{2,1,0:T(8,128)S(1)} collective-permute-done((f32[20,64,128]{2,1,0:T(8,128)S(1)}, f32[20,64,128]{2,1,0:T(8,128)S(1)}, u32[]{:S(2)}, u32[]{:S(2)}) %collective-permute-start) | collective-permute-done | bytes 655392 | tf_op jit(solution)/shard_map/while/body/eval_jaxpr/ppermute | solution.py:16
  380.1 15.1 %collective-permute-done = f32[20,64,128]{2,1,0:T(8,128)S(1)} collective-permute-done((f32[20,64,128]{2,1,0:T(8,128)S(1)}, f32[20,64,128]{2,1,0:T(8,128)S(1)}, u32[]{:S(2)}, u32[]{:S(2)}) %collective-permute-start) | collective-permute-done | bytes 655392 | tf_op jit(solution)/shard_map/while/body/eval_jaxpr/ppermute | solution.py:16
  396.6 14.2 %collective-permute-done = f32[20,64,128]{2,1,0:T(8,128)S(1)} collective-permute-done((f32[20,64,128]{2,1,0:T(8,128)S(1)}, f32[20,64,128]{2,1,0:T(8,128)S(1)}, u32[]{:S(2)}, u32[]{:S(2)}) %collective-permute-start) | collective-permute-done | bytes 655392 | tf_op jit(solution)/shard_map/while/body/eval_jaxpr/ppermute | solution.py:16
  412.2 13.2 %collective-permute-done = f32[20,64,128]{2,1,0:T(8,128)S(1)} collective-permute-done((f32[20,64,128]{2,1,0:T(8,128)S(1)}, f32[20,64,128]{2,1,0:T(8,128)S(1)}, u32[]{:S(2)}, u32[]{:S(2)}) %collective-permute-start) | collective-permute-done | bytes 655392 | tf_op jit(solution)/shard_map/while/body/eval_jaxpr/ppermute | solution.py:16
  426.8 12.3 %collective-permute-done = f32[20,64,128]{2,1,0:T(8,128)S(1)} collective-permute-done((f32[20,64,128]{2,1,0:T(8,128)S(1)}, f32[20,64,128]{2,1,0:T(8,128)S(1)}, u32[]{:S(2)}, u32[]{:S(2)}) %collective-permute-start) | collective-permute-done | bytes 655392 | tf_op jit(solution)/shard_map/while/body/eval_jaxpr/ppermute | solution.py:16
  440.6 11.8 %collective-permute-done = f32[20,64,128]{2,1,0:T(8,128)S(1)} collective-permute-done((f32[20,64,128]{2,1,0:T(8,128)S(1)}, f32[20,64,128]{2,1,0:T(8,128)S(1)}, u32[]{:S(2)}, u32[]{:S(2)}) %collective-permute-start) | collective-permute-done | bytes 655392 | tf_op jit(solution)/shard_map/while/body/eval_jaxpr/ppermute | solution.py:16
  452.4 5.5 %multiply_add_fusion.1 = f32[512,20,64]{0,2,1:T(8,128)} fusion(f32[512,20,64]{0,2,1:T(8,128)} %bitcast.122, f32[512,20,64]{0,2,1:T(8,128)} %reshape.102, f32[20,64,128]{2,1,0:T(8,128)S(1)} %get-tuple-element.72, f32[20]{0:T(128)S(1)} %copy-done.12, f32[512,20]{0,1:T(8,128)S(1)} %copy-done.6, bf16[512,1536]{1,0:T(8,128)(2,1)} %copy-done.3), kind=kOutput, calls=%fused_computation.67 | convolution fusion | flops 1009254400 | bytes 8691792 | tf_op jit(solution)/shard_map/tn,hpn->thp/dot_general | solution.py:132
  457.9 2.1 copy.65
  460.1 2.2 multiply_reduce_fusion
  462.3 9.2 %psum.7 = f32[512]{0:T(512)S(1)} all-reduce(f32[512]{0:T(512)S(1)} %multiply_reduce_fusion), channel_id=1, replica_groups=mesh['groups'=2,'seq'=8,'mp'=2] {'mp'}, use_global_device_ids=true, to_apply=%region_9.10 | all-reduce | flops 512 | bytes 4096 | tf_op jit(solution)/shard_map/psum | solution.py:137
  471.5 9.7 %fusion.43 = f32[512,2560]{1,0:T(8,128)} fusion(bf16[1280,2560]{0,1:T(8,128)(2,1)} %all-gather.9.cloned.1.call-done, f32[1280]{0:T(1024)S(1)} %copy-done.14, f32[512]{0:T(512)S(1)} %add_rsqrt_fusion, f32[512,1280]{1,0:T(8,128)S(1)} %copy.65, bf16[512,2560]{1,0:T(8,128)(2,1)} %convolution_convert_fusion), kind=kOutput, calls=%fused_computation.69 | convolution fusion | flops 3361341440 | bytes 15735808 | tf_op jit(solution)/shard_map/dot_general | solution.py:142
  481.3 15.6 %reduce-scatter.2.cloned.1.call-done = f32[512,1280]{1,0:T(8,128)} async-done(((f32[512,2560]{1,0:T(8,128)}), f32[512,1280]{1,0:T(8,128)}) %reduce-scatter.2.cloned.1.call-update) | async-done | bytes 2621456 | tf_op jit(solution)/shard_map/reduce_scatter | solution.py:147
  496.9 2.9 convert_element_type.50
  (135 shorter events, 34.8 us)
Async XLA Ops:
  6.5 27.0 %copy-start = (bf16[512,2560]{1,0:T(8,128)(2,1)S(1)}, bf16[512,2560]{1,0:T(8,128)(2,1)}, u32[]{:S(2)}) copy-start(bf16[512,2560]{1,0:T(8,128)(2,1)} %param.17) | copy-start | bytes 7864324
  6.5 2.3 copy-start.7
  6.5 2.3 copy-start.10
  6.5 2.4 copy-start.15
  6.5 2.4 copy-start.8
  6.5 27.0 %copy-start.13 = (f32[20]{0:T(128)S(1)}, f32[20]{0:T(128)}, u32[]{:S(2)}) copy-start(f32[20]{0:T(128)} %param.25) | copy-start | bytes 244
  6.6 43.0 %all-gather.7.cloned.1.call-start = ((), (), s32[]{:S(2)}) async-start(), calls=%async_computation.2 | async-start | bytes 1474560 | tf_op jit(solution)/shard_map/all_gather | solution.py:98
  7.3 226.4 %all-gather.5.cloned.1.call-start = ((), (), s32[]{:S(2)}) async-start(), calls=%async_computation.1 | async-start | bytes 14745600 | tf_op jit(solution)/shard_map/all_gather | solution.py:97
  8.0 463.5 %all-gather.9.cloned.1.call-start = ((), (), s32[]{:S(2)}) async-start(), calls=%async_computation.3 | async-start | bytes 7372800 | tf_op jit(solution)/shard_map/all_gather | solution.py:144
  8.8 488.1 %reduce-scatter.2.cloned.1.call-start = ((), (), s32[]{:S(2)}) async-start(), calls=%async_computation.4 | async-start | bytes 7864320 | tf_op jit(solution)/shard_map/reduce_scatter | solution.py:147
  250.3 3.0 copy-start.9
  250.3 3.0 copy-start.11
  251.8 4.8 collective-permute-start.1
  259.1 2.0 copy-start.3
  264.3 1.2 copy-start.4
  265.5 1.7 copy-start.5
  299.8 1.2 copy-start.4
  301.0 1.7 copy-start.5
  334.4 4.9 copy-start.2
  341.5 110.8 %copy-start.6 = (f32[512,20]{0,1:T(8,128)S(1)}, f32[512,20]{0,1:T(8,128)}, u32[]{:S(2)}) copy-start(f32[512,20]{0,1:T(8,128)} %bitcast_exponential_fusion.1) | copy-start | bytes 122884
  341.5 110.8 %copy-start.12 = (f32[20]{0:T(128)S(1)}, f32[20]{0:T(128)}, u32[]{:S(2)}) copy-start(f32[20]{0:T(128)} %param.27) | copy-start | bytes 244
  341.7 19.5 %collective-permute-start = (f32[20,64,128]{2,1,0:T(8,128)S(1)}, f32[20,64,128]{2,1,0:T(8,128)S(1)}, u32[]{:S(2)}, u32[]{:S(2)}) collective-permute-start(f32[20,64,128]{2,1,0:T(8,128)S(1)} %multiply_add_fusion.3), channel_id=1, source_target_pairs={{0,2},{2,4},{4,6},{6,8},{8,10},{10,12},{12,14},{1,3},{3,5},{5,7},{... | collective-permute-start | bytes 1966088 | tf_op jit(solution)/shard_map/while/body/eval_jaxpr/ppermute | solution.py:16
  361.3 17.3 %collective-permute-start = (f32[20,64,128]{2,1,0:T(8,128)S(1)}, f32[20,64,128]{2,1,0:T(8,128)S(1)}, u32[]{:S(2)}, u32[]{:S(2)}) collective-permute-start(f32[20,64,128]{2,1,0:T(8,128)S(1)} %multiply_add_fusion.3), channel_id=1, source_target_pairs={{0,2},{2,4},{4,6},{6,8},{8,10},{10,12},{12,14},{1,3},{3,5},{5,7},{... | collective-permute-start | bytes 1966088 | tf_op jit(solution)/shard_map/while/body/eval_jaxpr/ppermute | solution.py:16
  378.7 16.4 %collective-permute-start = (f32[20,64,128]{2,1,0:T(8,128)S(1)}, f32[20,64,128]{2,1,0:T(8,128)S(1)}, u32[]{:S(2)}, u32[]{:S(2)}) collective-permute-start(f32[20,64,128]{2,1,0:T(8,128)S(1)} %multiply_add_fusion.3), channel_id=1, source_target_pairs={{0,2},{2,4},{4,6},{6,8},{8,10},{10,12},{12,14},{1,3},{3,5},{5,7},{... | collective-permute-start | bytes 1966088 | tf_op jit(solution)/shard_map/while/body/eval_jaxpr/ppermute | solution.py:16
  395.3 15.5 %collective-permute-start = (f32[20,64,128]{2,1,0:T(8,128)S(1)}, f32[20,64,128]{2,1,0:T(8,128)S(1)}, u32[]{:S(2)}, u32[]{:S(2)}) collective-permute-start(f32[20,64,128]{2,1,0:T(8,128)S(1)} %multiply_add_fusion.3), channel_id=1, source_target_pairs={{0,2},{2,4},{4,6},{6,8},{8,10},{10,12},{12,14},{1,3},{3,5},{5,7},{... | collective-permute-start | bytes 1966088 | tf_op jit(solution)/shard_map/while/body/eval_jaxpr/ppermute | solution.py:16
  410.9 14.5 %collective-permute-start = (f32[20,64,128]{2,1,0:T(8,128)S(1)}, f32[20,64,128]{2,1,0:T(8,128)S(1)}, u32[]{:S(2)}, u32[]{:S(2)}) collective-permute-start(f32[20,64,128]{2,1,0:T(8,128)S(1)} %multiply_add_fusion.3), channel_id=1, source_target_pairs={{0,2},{2,4},{4,6},{6,8},{8,10},{10,12},{12,14},{1,3},{3,5},{5,7},{... | collective-permute-start | bytes 1966088 | tf_op jit(solution)/shard_map/while/body/eval_jaxpr/ppermute | solution.py:16
  425.5 13.6 %collective-permute-start = (f32[20,64,128]{2,1,0:T(8,128)S(1)}, f32[20,64,128]{2,1,0:T(8,128)S(1)}, u32[]{:S(2)}, u32[]{:S(2)}) collective-permute-start(f32[20,64,128]{2,1,0:T(8,128)S(1)} %multiply_add_fusion.3), channel_id=1, source_target_pairs={{0,2},{2,4},{4,6},{6,8},{8,10},{10,12},{12,14},{1,3},{3,5},{5,7},{... | collective-permute-start | bytes 1966088 | tf_op jit(solution)/shard_map/while/body/eval_jaxpr/ppermute | solution.py:16
  439.3 13.1 %collective-permute-start = (f32[20,64,128]{2,1,0:T(8,128)S(1)}, f32[20,64,128]{2,1,0:T(8,128)S(1)}, u32[]{:S(2)}, u32[]{:S(2)}) collective-permute-start(f32[20,64,128]{2,1,0:T(8,128)S(1)} %multiply_add_fusion.3), channel_id=1, source_target_pairs={{0,2},{2,4},{4,6},{6,8},{8,10},{10,12},{12,14},{1,3},{3,5},{5,7},{... | collective-permute-start | bytes 1966088 | tf_op jit(solution)/shard_map/while/body/eval_jaxpr/ppermute | solution.py:16
  460.0 11.5 %copy-start.14 = (f32[1280]{0:T(1024)S(1)}, f32[1280]{0:T(1024)}, u32[]{:S(2)}) copy-start(f32[1280]{0:T(1024)} %param.28) | copy-start | bytes 15364
  481.3 18.6 %copy-start.1 = (bf16[512,2560]{1,0:T(8,128)(2,1)S(1)}, bf16[512,2560]{1,0:T(8,128)(2,1)}, u32[]{:S(2)}) copy-start(bf16[512,2560]{1,0:T(8,128)(2,1)} %param.17) | copy-start | bytes 7864324
Sparse Core Ops, SparseCore 0:
  9.6 39.9 all-gather.6
  51.8 181.8 all-gather.4
  235.9 100.7 all-gather.8
  481.4 15.4 reduce-scatter.1
where the time goes:
time: 512 us; the launch traced here: 506 us
  waiting for transfers between devices  315 us (62%)
  local copies, waits for them, and re-layouts  83.2 us (16%)
  matrix products  35.1 us (7%)
  blocking collectives  33.6 us (7%)
  other arithmetic  14.7 us (3%)
  between operations  13.5 us (3%)
  starting transfers between devices  10.7 us (2%)
    all_gather x1, waiting for transfers between devices, shards(): lax.all_gather(zx_weight, 'seq', axis=0, tiled=True)  182 us
    ppermute x8, waiting for transfers between devices, shifted(): return lax.ppermute(block, axis, route)  103 us
    dynamic_update_slice x4, local copies, waits for them, and re-layouts, run_blocks(): lax.scan(block_step, start_state, (to_blocks(values), to_blocks(steps_dt)...  56.8 us
    all_gather x1, blocking collectives, shards(): lax.all_gather(dt_weight, 'seq', axis=0, tiled=True)  24.4 us
    reduce_scatter x1, waiting for transfers between devices, shards(): lax.psum_scatter(partial_out, 'mp', scatter_dimension=1, tiled=True)  15.6 us
    all_gather x1, waiting for transfers between devices, shards(): lax.all_gather(bc_weight, 'seq', axis=0, tiled=True)  12.8 us
    ppermute x8, starting transfers between devices, shifted(): return lax.ppermute(block, axis, route)  10.5 us
  transfers between devices with their start and end apart: 12, of which 11 were waited for; matrix products, arithmetic and copies ran while one was open for 24% of the time, Pallas kernels for 0%

commit v1 on v0

v1 whole, which is shorter than its diff:
```python
import jax
import jax.numpy as jnp
from jax import lax
from jax.experimental import pallas as pl
from jax.experimental.pallas import tpu as pltpu
from jax.sharding import PartitionSpec as P

STRETCH = 256
NORM_EPS = 1e-05
HEAD = 64
LANES = 128
BF16 = jnp.bfloat16
F32 = jnp.float32


def turned(block, axis, distance):
    size = lax.axis_size(axis)
    return lax.ppermute(block, axis, [(i, (i + distance) % size) for i in range(size)])


def shifted(block, axis, distance):
    size = lax.axis_size(axis)
    return lax.ppermute(block, axis, [(i, i + distance) for i in range(size - distance)])


def inner_kernel(values_ref, keys_ref, queries_ref, cum_ref, row_ref, y_ref):
    span = values_ref.shape[0]
    heads = cum_ref.shape[1]
    scores = lax.dot_general(
        queries_ref[...], keys_ref[...], (((1,), (1,)), ((), ())), preferred_element_type=F32
    )
    causal = lax.broadcasted_iota(jnp.int32, (span, span), 0) >= lax.broadcasted_iota(
        jnp.int32, (span, span), 1
    )
    for head in range(heads):
        across = cum_ref[:, head : head + 1] + row_ref[head : head + 1, :]
        decays = jnp.exp(jnp.where(causal, across, -jnp.inf))
        mixing = (decays * scores).astype(BF16)
        columns = slice(head * HEAD, (head + 1) * HEAD)
        y_ref[:, columns] = jnp.dot(mixing, values_ref[:, columns], preferred_element_type=F32)


def inner_blocks(values, keys_b, queries_c, cum, row):
    blocks, span, width = values.shape
    heads = cum.shape[2]
    state_dim = keys_b.shape[2]

    def spec(*shape):
        return pl.BlockSpec((None,) + shape, lambda b: (b, 0, 0))

    return pl.pallas_call(
        inner_kernel,
        grid=(blocks,),
        in_specs=[
            spec(span, width),
            spec(span, state_dim),
            spec(span, state_dim),
            spec(span, heads),
            spec(heads, span),
        ],
        out_specs=spec(span, width),
        out_shape=jax.ShapeDtypeStruct((blocks, span, width), F32),
        compiler_params=pltpu.CompilerParams(vmem_limit_bytes=32 * 2**20),
        cost_estimate=pl.CostEstimate(
            flops=2 * blocks * span * span * (width + state_dim),
            bytes_accessed=blocks * span * width * 6,
            transcendentals=blocks * heads * span * span,
        ),
    )(values, keys_b, queries_c, cum, row)


def shards(
    inputs,
    zx_weight,
    bc_weight,
    dt_weight,
    conv_x,
    conv_x_bias,
    conv_bc,
    conv_bc_bias,
    dt_bias,
    decay_log,
    skip_gain,
    norm_gain,
    out_weight,
):
    groups, seqs, cores = (lax.axis_size(a) for a in ("groups", "seq", "mp"))
    group, core = lax.axis_index("groups"), lax.axis_index("mp")
    rows, depth = inputs.shape
    slab = zx_weight.shape[0]
    taps, width_core = conv_x.shape
    heads_core = dt_weight.shape[1]
    width = width_core // groups
    heads = heads_core // groups
    state_dim = bc_weight.shape[1] // 2
    bc_width = 2 * state_dim // cores
    blocks = rows // STRETCH

    def mine(array, axis, size):
        return lax.dynamic_slice_in_dim(array, group * size, size, axis)

    tail = -(-(heads) // LANES) * LANES
    first = jnp.concatenate(
        [
            mine(zx_weight[:, 1, :], 1, width),
            lax.dynamic_slice_in_dim(bc_weight, core * bc_width, bc_width, 1),
            jnp.pad(mine(dt_weight, 1, heads), ((0, 0), (0, tail - heads))),
        ],
        axis=1,
    )
    first_all = lax.all_gather(first, "seq", axis=0, tiled=True)

    part = depth // cores
    own_part = lax.dynamic_slice_in_dim(inputs, core * part, part, 1)
    batches = [inputs]
    for d in range(1, groups):
        arrived = turned(own_part, "groups", d)
        joined = jnp.zeros((rows, depth), BF16)
        joined = lax.dynamic_update_slice_in_dim(joined, arrived, core * part, 1)
        for c in range(1, cores):
            other = turned(arrived, "mp", c)
            joined = lax.dynamic_update_slice_in_dim(
                joined, other, lax.rem(core + cores - c, cores) * part, 1
            )
        batches.append(joined)
    batch = jnp.concatenate(batches, axis=0)

    out_t, first_all = lax.optimization_barrier((mine(out_weight, 0, width).T, first_all))
    out_all = lax.all_gather(out_t, "seq", axis=0, tiled=True)
    z_own, out_all = lax.optimization_barrier((mine(zx_weight[:, 0, :], 1, width), out_all))
    z_all = lax.all_gather(z_own, "seq", axis=0, tiled=True)
    out_pieces = [out_all] + [turned(out_all, "groups", d) for d in range(1, groups)]

    summed = jnp.dot(batch, first_all, preferred_element_type=F32)
    raw_x = summed[:, :width].astype(BF16)
    raw_part = summed[:, width : width + bc_width].astype(BF16)
    dt_raw = summed[:, width + bc_width : width + bc_width + heads]
    raw_bc = jnp.zeros((groups * rows, 2 * state_dim), BF16)
    raw_bc = lax.dynamic_update_slice_in_dim(raw_bc, raw_part, core * bc_width, 1)
    for c in range(1, cores):
        raw_bc = lax.dynamic_update_slice_in_dim(
            raw_bc,
            turned(raw_part, "mp", c),
            lax.rem(core + cores - c, cores) * bc_width,
            1,
        )
    raw_all = jnp.concatenate([raw_x, raw_bc], axis=1).reshape(groups, rows, width + 2 * state_dim)
    rim_rows = shifted(raw_all[:, rows - (taps - 1) :], "seq", 1)
    padded = jnp.concatenate([rim_rows, raw_all], axis=1)
    kernel = jnp.concatenate([mine(conv_x, 1, width), conv_bc], axis=1)
    total = jnp.concatenate([mine(conv_x_bias, 0, width), conv_bc_bias])[None, None, :]
    for tap in range(taps):
        total = total + kernel[tap][None, None, :] * padded[:, tap : tap + rows].astype(F32)
    mixed_conv = jax.nn.silu(total).astype(BF16)

    batch_blocks = groups * blocks
    mixed_conv = mixed_conv.reshape(batch_blocks, STRETCH, width + 2 * state_dim)
    values = mixed_conv[:, :, :width]
    keys_b = mixed_conv[:, :, width : width + state_dim]
    queries_c = mixed_conv[:, :, width + state_dim :]
    steps_dt = jax.nn.softplus(dt_raw + mine(dt_bias, 0, heads)[None, :])
    log_decay = -jnp.exp(mine(decay_log, 0, heads))[None, :] * steps_dt
    steps_dt = steps_dt.reshape(batch_blocks, STRETCH, heads)
    cum = jnp.cumsum(log_decay.reshape(batch_blocks, STRETCH, heads), axis=1)
    cum_last = cum[:, -1, :]

    def wide(array):
        return jnp.repeat(array, HEAD, axis=-1)

    tail_decay = jnp.exp(cum_last[:, None, :] - cum) * steps_dt
    weighted = (wide(tail_decay) * values.astype(F32)).astype(BF16)
    block_states = jnp.einsum(
        "bsw,bsn->bwn", weighted, keys_b, preferred_element_type=F32
    ).reshape(groups, blocks, width, state_dim)
    block_decay = jnp.exp(cum_last).reshape(groups, blocks, heads)
    held = [jnp.zeros((groups, width, state_dim), F32)]
    passed = [jnp.ones((groups, heads), F32)]
    for b in range(blocks):
        held.append(wide(block_decay[:, b])[:, :, None] * held[-1] + block_states[:, b])
        passed.append(passed[-1] * block_decay[:, b])

    def packed(state, decay):
        high = decay.astype(BF16)
        low = (decay - high.astype(F32)).astype(BF16)
        extra = jnp.stack([high, low], axis=1)
        extra = jnp.pad(extra, ((0, 0), (0, 14), (0, state_dim - heads)))
        return jnp.concatenate([state.astype(BF16), extra], axis=1)

    def unpacked(message):
        decay = message[:, width, :heads].astype(F32) + message[:, width + 1, :heads].astype(F32)
        return message[:, :width].astype(F32), decay

    message = packed(held[-1], passed[-1])
    state, decay = unpacked(shifted(message, "seq", 1))
    if seqs > 2:
        far_state, far_decay = unpacked(shifted(message, "seq", 2))
        state = state + wide(decay)[:, :, None] * far_state
        decay = decay * far_decay
    reach = 2
    while reach < seqs - 1:
        far_state, far_decay = unpacked(shifted(packed(state, decay), "seq", reach))
        state = state + wide(decay)[:, :, None] * far_state
        decay = decay * far_decay
        reach *= 2

    inner = inner_blocks(
        values, keys_b, queries_c, cum, (jnp.log(steps_dt) - cum).transpose(0, 2, 1)
    )

    gate_z = jnp.dot(batch, z_all, preferred_element_type=F32).astype(BF16)

    state_in = jnp.stack(
        [held[b] + wide(passed[b])[:, :, None] * state for b in range(blocks)], axis=1
    ).reshape(batch_blocks, width, state_dim)
    entering = jnp.einsum(
        "bsn,bwn->bsw", queries_c, state_in.astype(BF16), preferred_element_type=F32
    )
    skip = wide(mine(skip_gain, 0, heads))[None, None, :]
    output_y = inner + wide(jnp.exp(cum)) * entering + skip * values.astype(F32)
    gated = output_y.reshape(groups, rows, width) * jax.nn.silu(
        gate_z.astype(F32).reshape(groups, rows, width)
    )
    squares = jnp.sum(gated * gated, axis=2)
    scaled = (gated * mine(norm_gain, 0, width)[None, None, :]).astype(BF16)

    partial = jnp.zeros((rows, seqs * out_weight.shape[1]), F32)
    square = jnp.zeros((rows,), F32)
    for d in range(groups):
        at = (-d) % groups
        piece, square_piece = scaled[at], squares[at]
        if d:
            piece, square_piece = turned(piece, "groups", d), turned(square_piece, "groups", d)
        partial = partial + lax.dot_general(
            piece, out_pieces[d], (((1,), (1,)), ((), ())), preferred_element_type=F32
        )
        square = square + square_piece
    columns = partial.shape[1] // cores
    mixed = lax.dynamic_slice_in_dim(partial, core * columns, columns, 1)
    total_square = square
    for c in range(1, cores):
        theirs = lax.dynamic_slice_in_dim(
            partial, lax.rem(core + c, cores) * columns, columns, 1
        ).astype(BF16)
        mixed = mixed + turned(theirs, "mp", c).astype(F32)
        total_square = total_square + turned(square, "mp", c)
    mean_square = total_square / (width_core * cores)
    return (mixed * lax.rsqrt(mean_square + NORM_EPS)[:, None]).astype(BF16)


def solution(mesh):
    return jax.shard_map(
        shards,
        mesh=mesh,
        in_specs=(
            P(("groups", "seq"), None),
            P("seq", None, "mp"),
            P("seq", None),
            P("seq", "mp"),
            P(None, "mp"),
            P("mp"),
            P(),
            P(),
            P("mp"),
            P("mp"),
            P("mp"),
            P("mp"),
            P("mp", "seq"),
        ),
        out_specs=P(("groups", "seq"), "mp"),
        check_vma=False,
    )
```

time: 512 us -> 365 us (0.71)
  waiting for transfers between devices: 315 us -> 238 us
  local copies, waits for them, and re-layouts: 83.2 us -> 33.8 us
  blocking collectives: 33.6 us -> 0 us
  other arithmetic: 14.7 us -> 33.9 us
  matrix products: 35.1 us -> 25.4 us
    all_gather x3, waiting for transfers between devices: 195 us -> 108 us  [the longest x1 72.1 us: shards(): first_all = lax.all_gather(first, 'seq', axis=0, tiled=True)]
    dynamic_update_slice x4 -> x3, local copies, waits for them, and re-layouts: 56.8 us -> 3.77 us  [the longest x1 2.14 us: shards(): lax.dynamic_update_slice_in_dim(joined, other, lax.rem(core + cores - c,...]
    ppermute x8 -> x13, waiting for transfers between devices: 103 us -> 129 us  [the longest x8 69.3 us: turned(): lax.ppermute(block, axis, [(i, (i + distance) % size) for i in range(size)])]
    all_gather x1 -> x0, blocking collectives: 24.4 us -> none  [shards(): lax.all_gather(dt_weight, 'seq', axis=0, tiled=True)]
    reduce_scatter x1 -> x0, waiting for transfers between devices: 15.6 us -> none  [shards(): lax.psum_scatter(partial_out, 'mp', scatter_dimension=1, tiled=True)]
    convert_element_type x3 -> x8, other arithmetic: 5.42 us -> 17.9 us  [the longest x3 8.71 us: packed(): return jnp.concatenate([state.astype(BF16), extra], axis=1)]
    dot_general x13 -> x6, matrix products: 35.1 us -> 25.4 us  [the longest x2 8.38 us: shards(): lax.dot_general(piece, out_pieces[d], (((1,), (1,)), ((), ())), preferred...]
    psum x1 -> x0, blocking collectives: 9.23 us -> none  [shards(): total_square = lax.psum(jnp.sum(gated * gated, axis=1), 'mp')]
  transfers between devices with their start and end apart: 12 -> 16, of which waited for: 11 -> 9; matrix products, arithmetic and copies ran while one was open for 24% -> 21% of each run, Pallas kernels for 0% -> 1%
where the time goes in v1:
time: 365 us; the launch traced here: 362 us
  waiting for transfers between devices  238 us (65%)
  other arithmetic  33.9 us (9%)
  local copies, waits for them, and re-layouts  33.8 us (9%)
  matrix products  25.4 us (7%)
  starting transfers between devices  14.4 us (4%)
  between operations  13.8 us (4%)
    all_gather x1, waiting for transfers between devices, shards(): first_all = lax.all_gather(first, 'seq', axis=0, tiled=True)  72.1 us
    ppermute x8, waiting for transfers between devices, turned(): lax.ppermute(block, axis, [(i, (i + distance) % size) for i in range(size)])  69.3 us
    ppermute x5, waiting for transfers between devices, shifted(): lax.ppermute(block, axis, [(i, i + distance) for i in range(size - distan...  59.9 us
    all_gather x1, waiting for transfers between devices, shards(): out_all = lax.all_gather(out_t, 'seq', axis=0, tiled=True)  36.3 us
    convert_element_type x3, other arithmetic, packed(): return jnp.concatenate([state.astype(BF16), extra], axis=1)  8.71 us
    dot_general x2, matrix products, shards(): lax.dot_general(piece, out_pieces[d], (((1,), (1,)), ((), ())), preferred...  8.38 us
    dot_general x1, matrix products, shards(): gate_z = jnp.dot(batch, z_all, preferred_element_type=F32).astype(BF16)  8.3 us
    ppermute x8, starting transfers between devices, turned(): lax.ppermute(block, axis, [(i, (i + distance) % size) for i in range(size)])  7.44 us
  transfers between devices with their start and end apart: 16, of which 9 were waited for; matrix products, arithmetic and copies ran while one was open for 21% of the time, Pallas kernels for 1%

profile of v1, /device:TPU:29, one launch (start us, length us, event | category | flops | bytes accessed | tf_op | source)
XLA Modules:
  0.0 362.4 jit_solution(1567096855408420715)
XLA Ops:
  6.5 5.6 %fusion.58 = (bf16[320,1,1280]{2,1,0:T(2,128)(2,1)}, bf16[320,1,1280]{2,1,0:T(2,128)(2,1)S(1)}) fusion(bf16[320,2,1280]{2,1,0:T(2,128)(2,1)} %param.14), kind=kLoop, calls=%fused_computation.128 | loop fusion | bytes 3276800 | tf_op jit(solution)/shard_map/slice | solution.py:105
  12.3 2.0 constant_dynamic-slice_fusion.3
  15.4 2.5 constant_dynamic-slice_fusion.4
  20.0 72.1 %all-gather.4.cloned.1.call-done = bf16[2560,896]{1,0:T(8,128)(2,1)} async-done(((bf16[320,896]{1,0:T(8,128)(2,1)}), bf16[2560,896]{1,0:T(8,128)(2,1)}) %all-gather.4.cloned.1.call-update) | async-done | bytes 4587536 | tf_op jit(solution)/shard_map/all_gather | solution.py:111
  94.9 1.6 constant_dynamic-update-slice_fusion.3
  96.5 2.1 constant_dynamic-update-slice_fusion.2
  98.7 5.1 %fusion.61 = (bf16[1024,896]{0,1:T(8,128)(2,1)S(1)}, f32[1024,896]{0,1:T(8,128)S(1)}) fusion(bf16[2560,896]{1,0:T(8,128)(2,1)S(1)} %copy-done.22, bf16[512,2560]{1,0:T(8,128)(2,1)S(1)} %constant_dynamic-update-slice_fusion.2, bf16[512,2560]{1,0:T(8,128)(2,1)S(1)} %copy-done.13), kind=kOutput, calls=%fused_computation.131 | convolution fusion | flops 4709023744 | bytes 15335424 | tf_op jit(solution)/shard_map/dot_general | solution.py:134
  105.4 2.3 reduce-window.6
  109.8 1.5 pad_maximum_fusion.4
  111.3 3.1 copy.63
  114.4 1.5 collective-permute-start.3
  116.1 2.1 copy.49
  118.5 36.3 %all-gather.6.cloned.1.call-done = bf16[2560,640]{1,0:T(8,128)(2,1)} async-done(((bf16[320,640]{1,0:T(8,128)(2,1)}), bf16[2560,640]{1,0:T(8,128)(2,1)}) %all-gather.6.cloned.1.call-update) | async-done | bytes 3276816 | tf_op jit(solution)/shard_map/all_gather | solution.py:129
  154.8 6.4 %multiply_convert_fusion = bf16[2,512,896]{2,1,0:T(8,128)(2,1)S(1)} fusion(bf16[2,512,896]{2,1,0:T(8,128)(2,1)} %bitcast.106, bf16[2,3,896]{2,1,0:T(4,128)(2,1)S(1)} %collective-permute-done.3, f32[896]{0:T(1024)S(1)} %get-tuple-element.17, f32[896]{0:T(1024)S(1)} %get-tuple-element.18, f32[896]{0:T(1024)S(1)} %get-tuple-element.16, ...), kind=kLoop, calls=%fused_computation.2 | loop fusion | flops 23855104 | bytes 3698688 | tf_op jit(solution)/shard_map/convert_element_type | solution.py:154
  162.1 2.9 fusion.15
  167.9 20.4 %collective-permute-done.5 = bf16[2,656,128]{2,0,1:T(2,128)(2,1)S(1)} collective-permute-done((bf16[2,656,128]{2,0,1:T(2,128)(2,1)S(1)}, bf16[2,656,128]{2,0,1:T(2,128)(2,1)S(1)}, u32[]{:S(2)}, u32[]{:S(2)}) %collective-permute-start.5) | collective-permute-done | bytes 335904 | tf_op jit(solution)/shard_map/ppermute | solution.py:23
  189.2 1.8 fusion.18
  192.7 30.4 %collective-permute-done.6 = bf16[2,656,128]{2,0,1:T(2,128)(2,1)S(1)} collective-permute-done((bf16[2,656,128]{2,0,1:T(2,128)(2,1)S(1)}, bf16[2,656,128]{2,0,1:T(2,128)(2,1)S(1)}, u32[]{:S(2)}, u32[]{:S(2)}) %collective-permute-start.6) | collective-permute-done | bytes 335904 | tf_op jit(solution)/shard_map/ppermute | solution.py:23
  225.3 4.0 %fusion.53 = (bf16[2,640,128]{2,0,1:T(2,128)(2,1)S(1)}, f32[2,640,128]{2,0,1:T(2,128)}) fusion(bf16[2,656,128]{2,0,1:T(2,128)(2,1)} %copy-done.14, f32[2,640]{0,1:T(8,128)S(1)} %bitcast.115, bf16[2,656,128]{2,0,1:T(2,128)(2,1)S(1)} %collective-permute-done.5, f32[2,640]{0,1:T(8,128)S(1)} %bitcast.109, bf16[2,656,128]{2,0,1:T(2,128)(2,1)} %copy-done.12), kind=kLoop, calls=%fused_computation.125 | loop fusion | flops 1310720 | bytes 1976320 | tf_op jit(solution)/shard_map/convert_element_type | solution.py:187
  230.5 1.5 collective-permute-start.7
  232.5 1.7 broadcast_in_dim.41
  234.2 3.3 copy.58
  237.7 3.6 shard_map.127
  241.4 9.1 %collective-permute-done.7 = bf16[2,656,128]{2,0,1:T(2,128)(2,1)} collective-permute-done((bf16[2,656,128]{2,0,1:T(2,128)(2,1)}, bf16[2,656,128]{2,0,1:T(2,128)(2,1)}, u32[]{:S(2)}, u32[]{:S(2)}) %collective-permute-start.7) | collective-permute-done | bytes 335904 | tf_op jit(solution)/shard_map/ppermute | solution.py:23
  250.6 6.2 %convert_bitcast_fusion = (bf16[2,1,640,128]{3,0,2,1:T(2,128)(2,1)S(1)}, bf16[2,1,640,128]{3,0,2,1:T(2,128)(2,1)S(1)}) fusion(f32[2,640,128]{2,0,1:T(2,128)} %get-tuple-element.24, bf16[2,656,128]{2,0,1:T(2,128)(2,1)} %collective-permute-done.7, f32[2,640]{0,1:T(8,128)S(1)} %bitcast.113, f32[2,640]{0,1:T(8,128)S(1)} %bitcast.114, ...), kind=kLoop, calls=%fused_computation.48 | loop fusion | flops 1310720 | bytes 2309120 | tf_op jit(solution)/shard_map/stack | solution.py:212
  259.1 2.9 fusion.48
  262.0 8.3 %fusion.9 = f32[1024,640]{1,0:T(8,128)S(1)} fusion(bf16[2560,640]{1,0:T(8,128)(2,1)} %all-gather.8.cloned.1.call-done, bf16[512,2560]{1,0:T(8,128)(2,1)} %copy-done.10, bf16[512,2560]{1,0:T(8,128)(2,1)} %param.13), kind=kOutput, calls=%fused_computation.22 | convolution fusion | flops 3367239680 | bytes 11141120 | tf_op jit(solution)/shard_map/dot_general | solution.py:210
  272.7 4.2 %fusion.13 = f32[512,2560]{1,0:T(8,128)S(1)} fusion(bf16[2560,640]{1,0:T(8,128)(2,1)} %all-gather.6.cloned.1.call-done, bf16[2,512,640]{2,1,0:T(8,128)(2,1)S(1)} %fusion.5), kind=kOutput, calls=%fused_computation.29 | convolution fusion | flops 1677721600 | bytes 9175040 | tf_op jit(solution)/shard_map/dot_general | solution.py:233
  276.9 53.3 %collective-permute-done.9 = bf16[2560,640]{1,0:T(8,128)(2,1)} collective-permute-done((bf16[2560,640]{1,0:T(8,128)(2,1)}, bf16[2560,640]{1,0:T(8,128)(2,1)}, u32[]{:S(2)}, u32[]{:S(2)}) %collective-permute-start.9) | collective-permute-done | bytes 3276832 | tf_op jit(solution)/shard_map/ppermute | solution.py:18
  330.1 13.9 %collective-permute-done.8 = bf16[512,640]{1,0:T(8,128)(2,1)S(1)} collective-permute-done((bf16[512,640]{1,0:T(8,128)(2,1)S(1)}, bf16[512,640]{1,0:T(8,128)(2,1)S(1)}, u32[]{:S(2)}, u32[]{:S(2)}) %collective-permute-start.8) | collective-permute-done | bytes 655392 | tf_op jit(solution)/shard_map/ppermute | solution.py:18
  344.1 4.2 %convolution_add_fusion = f32[512,2560]{1,0:T(8,128)S(1)} fusion(f32[512,2560]{1,0:T(8,128)S(1)} %fusion.13, bf16[512,640]{1,0:T(8,128)(2,1)S(1)} %collective-permute-done.8, bf16[2560,640]{1,0:T(8,128)(2,1)} %collective-permute-done.9), kind=kOutput, calls=%fused_computation.1 | convolution fusion | flops 1679032320 | bytes 14417920 | tf_op jit(solution)/shard_map/dot_general | solution.py:233
  348.5 1.5 collective-permute-start.10
  (156 shorter events, 31.4 us)
Async XLA Ops:
  6.5 12.6 %copy-start = (bf16[1280,320]{0,1:T(8,128)(2,1)S(1)}, bf16[1280,320]{0,1:T(8,128)(2,1)}, u32[]{:S(2)}) copy-start(bf16[1280,320]{0,1:T(8,128)(2,1)} %param.25) | copy-start | bytes 2457604
  6.5 85.5 %all-gather.4.cloned.1.call-start = ((), (), s32[]{:S(2)}) async-start(), calls=%async_computation | async-start | bytes 5160960 | tf_op jit(solution)/shard_map/all_gather | solution.py:111
  15.3 139.4 %all-gather.6.cloned.1.call-start = ((), (), s32[]{:S(2)}) async-start(), calls=%async_computation.1 | async-start | bytes 3686400 | tf_op jit(solution)/shard_map/all_gather | solution.py:129
  17.9 76.5 %copy-start.19 = (f32[1280]{0:T(1024)S(1)}, f32[1280]{0:T(1024)}, u32[]{:S(2)}) copy-start(f32[1280]{0:T(1024)} %param.18) | copy-start | bytes 15364
  17.9 76.6 %copy-start.23 = (f32[20]{0:T(128)S(1)}, f32[20]{0:T(128)}, u32[]{:S(2)}) copy-start(f32[20]{0:T(128)} %param.21) | copy-start | bytes 244
  17.9 76.7 %copy-start.17 = (f32[4,1280]{1,0:T(4,128)S(1)}, f32[4,1280]{1,0:T(4,128)}, u32[]{:S(2)}) copy-start(f32[4,1280]{1,0:T(4,128)} %param.17) | copy-start | bytes 61444
  17.9 76.7 %copy-start.18 = (f32[4,256]{1,0:T(4,128)S(1)}, f32[4,256]{1,0:T(4,128)}, u32[]{:S(2)}) copy-start(f32[4,256]{1,0:T(4,128)} %param.19) | copy-start | bytes 12292
  17.9 76.7 %copy-start.24 = (f32[20]{0:T(128)S(1)}, f32[20]{0:T(128)}, u32[]{:S(2)}) copy-start(f32[20]{0:T(128)} %param.22) | copy-start | bytes 244
  17.9 76.8 %copy-start.21 = (f32[256]{0:T(256)S(1)}, f32[256]{0:T(256)}, u32[]{:S(2)}) copy-start(f32[256]{0:T(256)} %param.20) | copy-start | bytes 3076
  17.9 74.2 %collective-permute-start = (bf16[512,1280]{1,0:T(8,128)(2,1)}, bf16[512,1280]{1,0:T(8,128)(2,1)}, u32[]{:S(2)}, u32[]{:S(2)}) collective-permute-start(bf16[512,1280]{1,0:T(8,128)(2,1)} %constant_dynamic-slice_fusion.4), channel_id=1, source_target_pairs={{0,16},{16,0},{1,17},{17,1},{2,18},{18,2},{3,19},{19,3},{4,20},{20... | collective-permute-start | bytes 3932168 | tf_op jit(solution)/shard_map/ppermute | solution.py:18
  92.1 169.9 %all-gather.8.cloned.1.call-start = ((), (), s32[]{:S(2)}) async-start(), calls=%async_computation.2 | async-start | bytes 3686400 | tf_op jit(solution)/shard_map/all_gather | solution.py:131
  92.1 4.4 %collective-permute-start.1 = (bf16[512,1280]{1,0:T(8,128)(2,1)}, bf16[512,1280]{1,0:T(8,128)(2,1)}, u32[]{:S(2)}, u32[]{:S(2)}) collective-permute-start(bf16[512,1280]{1,0:T(8,128)(2,1)} %collective-permute-done), channel_id=1, source_target_pairs={{0,1},{1,0},{2,3},{3,2},{4,5},{5,4},{6,7},{7,6},{8,9},{9,8},{10,11... | collective-permute-start | bytes 3932168 | tf_op jit(solution)/shard_map/ppermute | solution.py:18
  105.1 4.7 %collective-permute-start.2 = (bf16[1024,128]{0,1:T(8,128)(2,1)S(1)}, bf16[1024,128]{0,1:T(8,128)(2,1)S(1)}, u32[]{:S(2)}, u32[]{:S(2)}) collective-permute-start(bf16[1024,128]{0,1:T(8,128)(2,1)S(1)} %get-tuple-element.34), channel_id=1, source_target_pairs={{0,1},{1,0},{2,3},{3,2},{4,5},{5,4},{6,7},{7,6},{8,9},{9,8},{10,11... | collective-permute-start | bytes 786440 | tf_op jit(solution)/shard_map/ppermute | solution.py:18
  114.4 40.4 %collective-permute-start.3 = (bf16[2,3,896]{2,1,0:T(4,128)(2,1)S(1)}, bf16[2,3,896]{2,1,0:T(4,128)(2,1)S(1)}, u32[]{:S(2)}, u32[]{:S(2)}) collective-permute-start(bf16[2,3,896]{2,1,0:T(4,128)(2,1)S(1)} %slice.158), channel_id=1, source_target_pairs={{0,2},{2,4},{4,6},{6,8},{8,10},{10,12},{12,14},{1,3},{3,5},{5,7},{... | collective-permute-start | bytes 32264 | tf_op jit(solution)/shard_map/ppermute | solution.py:23
  118.4 43.7 %copy-start.9 = (f32[2,640]{0,1:T(8,128)}, f32[2,640]{0,1:T(8,128)S(1)}, u32[]{:S(2)}) copy-start(f32[2,640]{0,1:T(8,128)S(1)} %bitcast_multiply_fusion.1) | copy-start | bytes 15364
  154.8 6.4 %copy-start.4 = (f32[4,256,640]{2,1,0:T(8,128)S(1)}, f32[4,256,640]{2,1,0:T(8,128)}, u32[]{:S(2)}) copy-start(f32[4,256,640]{2,1,0:T(8,128)} %copy.49) | copy-start | bytes 7864324
  161.2 76.4 %copy-start.2 = (bf16[2,512,896]{2,1,0:T(8,128)(2,1)}, bf16[2,512,896]{2,1,0:T(8,128)(2,1)S(1)}, u32[]{:S(2)}) copy-start(bf16[2,512,896]{2,1,0:T(8,128)(2,1)S(1)} %multiply_convert_fusion) | copy-start | bytes 5505028
  162.0 29.4 %copy-start.8 = (f32[2,1,640,128]{3,2,1,0:T(8,128)}, f32[2,1,640,128]{3,2,1,0:T(8,128)S(1)}, u32[]{:S(2)}) copy-start(f32[2,1,640,128]{3,2,1,0:T(8,128)S(1)} %get-tuple-element.41) | copy-start | bytes 1966084
  165.3 23.0 %collective-permute-start.5 = (bf16[2,656,128]{2,0,1:T(2,128)(2,1)S(1)}, bf16[2,656,128]{2,0,1:T(2,128)(2,1)S(1)}, u32[]{:S(2)}, u32[]{:S(2)}) collective-permute-start(bf16[2,656,128]{2,0,1:T(2,128)(2,1)S(1)} %fusion.19), channel_id=1, source_target_pairs={{0,4},{2,6},{4,8},{6,10},{8,12},{10,14},{1,5},{3,7},{5,9},{7,11},{... | collective-permute-start | bytes 1007624 | tf_op jit(solution)/shard_map/ppermute | solution.py:23
  166.6 21.7 %collective-permute-start.4 = (bf16[2,656,128]{2,0,1:T(2,128)(2,1)S(1)}, bf16[2,656,128]{2,0,1:T(2,128)(2,1)S(1)}, u32[]{:S(2)}, u32[]{:S(2)}) collective-permute-start(bf16[2,656,128]{2,0,1:T(2,128)(2,1)S(1)} %fusion.19), channel_id=1, source_target_pairs={{0,2},{2,4},{4,6},{6,8},{8,10},{10,12},{12,14},{1,3},{3,5},{5,7},{... | collective-permute-start | bytes 1007624 | tf_op jit(solution)/shard_map/ppermute | solution.py:23
  189.2 42.8 %copy-start.20 = (f32[1280]{0:T(1024)S(1)}, f32[1280]{0:T(1024)}, u32[]{:S(2)}) copy-start(f32[1280]{0:T(1024)} %param.24) | copy-start | bytes 15364
  189.2 42.9 %copy-start.25 = (f32[20]{0:T(128)S(1)}, f32[20]{0:T(128)}, u32[]{:S(2)}) copy-start(f32[20]{0:T(128)} %param.23) | copy-start | bytes 244
  191.4 31.7 %collective-permute-start.6 = (bf16[2,656,128]{2,0,1:T(2,128)(2,1)S(1)}, bf16[2,656,128]{2,0,1:T(2,128)(2,1)S(1)}, u32[]{:S(2)}, u32[]{:S(2)}) collective-permute-start(bf16[2,656,128]{2,0,1:T(2,128)(2,1)S(1)} %pad_maximum_fusion.10), channel_id=1, source_target_pairs={{0,4},{2,6},{4,8},{6,10},{8,12},{10,14},{1,5},{3,7},{5,9},{7,11},{... | collective-permute-start | bytes 1007624 | tf_op jit(solution)/shard_map/ppermute | solution.py:23
  230.5 20.1 %collective-permute-start.7 = (bf16[2,656,128]{2,0,1:T(2,128)(2,1)}, bf16[2,656,128]{2,0,1:T(2,128)(2,1)}, u32[]{:S(2)}, u32[]{:S(2)}) collective-permute-start(bf16[2,656,128]{2,0,1:T(2,128)(2,1)} %pad_maximum_fusion.11), channel_id=1, source_target_pairs={{0,8},{2,10},{4,12},{6,14},{1,9},{3,11},{5,13},{7,15},{16,24},{18,... | collective-permute-start | bytes 1007624 | tf_op jit(solution)/shard_map/ppermute | solution.py:23
  257.8 72.3 %collective-permute-start.9 = (bf16[2560,640]{1,0:T(8,128)(2,1)}, bf16[2560,640]{1,0:T(8,128)(2,1)}, u32[]{:S(2)}, u32[]{:S(2)}) collective-permute-start(bf16[2560,640]{1,0:T(8,128)(2,1)} %all-gather.6.cloned.1.call-done), channel_id=1, source_target_pairs={{0,16},{16,0},{1,17},{17,1},{2,18},{18,2},{3,19},{19,3},{4,20},{20... | collective-permute-start | bytes 9830408 | tf_op jit(solution)/shard_map/ppermute | solution.py:18
  262.0 8.3 %copy-start.3 = (bf16[2,512,896]{2,1,0:T(8,128)(2,1)S(1)}, bf16[2,512,896]{2,1,0:T(8,128)(2,1)}, u32[]{:S(2)}) copy-start(bf16[2,512,896]{2,1,0:T(8,128)(2,1)} %copy-done.2) | copy-start | bytes 5505028
  262.0 8.3 %copy-start.5 = (f32[4,256,640]{2,1,0:T(8,128)S(1)}, f32[4,256,640]{2,1,0:T(8,128)}, u32[]{:S(2)}) copy-start(f32[4,256,640]{2,1,0:T(8,128)} %copy.58) | copy-start | bytes 7864324
  262.0 8.3 %copy-start.6 = (f32[4,256,640]{2,1,0:T(8,128)S(1)}, f32[4,256,640]{2,1,0:T(8,128)}, u32[]{:S(2)}) copy-start(f32[4,256,640]{2,1,0:T(8,128)} %fusion.48) | copy-start | bytes 7864324
  272.4 71.7 %collective-permute-start.8 = (bf16[512,640]{1,0:T(8,128)(2,1)S(1)}, bf16[512,640]{1,0:T(8,128)(2,1)S(1)}, u32[]{:S(2)}, u32[]{:S(2)}) collective-permute-start(bf16[512,640]{1,0:T(8,128)(2,1)S(1)} %slice_bitcast_fusion), channel_id=1, source_target_pairs={{0,16},{16,0},{1,17},{17,1},{2,18},{18,2},{3,19},{19,3},{4,20},{20... | collective-permute-start | bytes 1966088 | tf_op jit(solution)/shard_map/ppermute | solution.py:18
  348.5 6.0 %collective-permute-start.10 = (bf16[512,1280]{1,0:T(8,128)(2,1)S(1)}, bf16[512,1280]{1,0:T(8,128)(2,1)S(1)}, u32[]{:S(2)}, u32[]{:S(2)}) collective-permute-start(bf16[512,1280]{1,0:T(8,128)(2,1)S(1)} %dynamic-slice_convert_fusion), channel_id=1, source_target_pairs={{0,1},{1,0},{2,3},{3,2},{4,5},{5,4},{6,7},{7,6},{8,9},{9,8},{10,11... | collective-permute-start | bytes 3932168 | tf_op jit(solution)/shard_map/ppermute | solution.py:18
  350.0 2.5 collective-permute-start.11
  352.4 2.0 collective-permute-start.12
  (10 other events, 26.5 us)
Sparse Core Ops, SparseCore 0:
  15.5 76.5 all-gather.3
  94.2 60.4 all-gather.5
  157.0 75.1 all-gather.7

commit v2 on v1

--- a/solution.py
+++ b/solution.py
@@ -1,3 +1,5 @@
+import functools
+
 import jax
 import jax.numpy as jnp
 from jax import lax
@@ -67,6 +69,177 @@
             transcendentals=blocks * heads * span * span,
         ),
     )(values, keys_b, queries_c, cum, row)
+
+MESH_ID = pl.DeviceIdType.MESH
+
+
+def gather_kernel(sizes, first_ref, out_ref, z_ref, x_ref, first_all, out_all, z_all, arrived, *sems):
+    groups, seqs, cores = sizes
+    ring_send, ring_recv, side_send, side_recv, x_send, x_recv, core_send, core_recv, own_sem = sems
+    group, seq, core = (lax.axis_index(a) for a in ("groups", "seq", "mp"))
+    odd = lax.rem(seq, 2)
+    half_at = lax.div(seq, 2)
+    place = (1 - odd) * half_at + odd * (seqs - 1 - half_at)
+
+    def seq_at(position):
+        position = lax.rem(position + 2 * seqs, seqs)
+        back = lax.div(position, seqs // 2)
+        return (1 - back) * 2 * position + back * (2 * (seqs - 1 - position) + 1)
+
+    def group_at(d):
+        return lax.rem(group + d, groups)
+
+    def core_at(c):
+        return lax.rem(core + c, cores)
+
+    barrier = pltpu.get_barrier_semaphore()
+    near = [{"seq": seq_at(place + 1)}, {"seq": seq_at(place - 1)}]
+    near += [{"groups": group_at(d)} for d in range(1, groups)]
+    near += [{"mp": core_at(c)} for c in range(1, cores)]
+    for other in near:
+        pl.semaphore_signal(barrier, inc=1, device_id=other, device_id_type=MESH_ID)
+    pl.semaphore_wait(barrier, len(near))
+
+    part = x_ref.shape[1] // cores
+    columns = pl.ds(pl.multiple_of(core * part, 128), part)
+    x_copies = []
+    for d in range(1, groups):
+        x_copies.append(
+            pltpu.make_async_remote_copy(
+                src_ref=x_ref.at[:, columns],
+                dst_ref=arrived.at[d - 1, :, columns],
+                send_sem=x_send.at[d - 1],
+                recv_sem=x_recv.at[d - 1],
+                device_id={"groups": group_at(d)},
+                device_id_type=MESH_ID,
+            )
+        )
+    for copy in x_copies:
+        copy.start()
+
+    owns = [first_ref, out_ref.at[0], z_ref]
+    alls = [first_all, out_all.at[0], z_all]
+    locals_ = [(first_ref, first_all.at[seq]), (z_ref, z_all.at[seq])]
+    locals_ += [(out_ref.at[d], out_all.at[d, seq]) for d in range(groups)]
+    own_copies = [
+        pltpu.make_async_copy(source, target, own_sem.at[i])
+        for i, (source, target) in enumerate(locals_)
+    ]
+
+    slab = first_ref.shape[0]
+    cut = (slab // 2 + 15) // 16 * 16
+    spans = [pl.ds(0, cut), pl.ds(cut, slab - cut)]
+    steps = seqs // 2
+    counts = [[steps, seqs - 1 - steps], [seqs - 1 - steps, steps]]
+    everything, sides, core_copies = [], [], []
+
+    def ring_copy(k, half, way, step):
+        owner = seq_at(place - step if way == 0 else place + step)
+        source = owns[k] if step == 0 else alls[k].at[owner]
+        return pltpu.make_async_remote_copy(
+            src_ref=source.at[spans[half]],
+            dst_ref=alls[k].at[owner, spans[half]],
+            send_sem=ring_send.at[k, half, way, step],
+            recv_sem=ring_recv.at[k, half, way, step],
+            device_id={"seq": seq_at(place + 1 if way == 0 else place - 1)},
+            device_id_type=MESH_ID,
+        )
+
+    def received(k, half, way, step, copy):
+        copy.wait_recv()
+        if k != 1:
+            return
+        owner = seq_at(place - 1 - step if way == 0 else place + 1 + step)
+        for d in range(1, groups):
+            side = pltpu.make_async_remote_copy(
+                src_ref=out_all.at[0, owner, spans[half]],
+                dst_ref=out_all.at[d, owner, spans[half]],
+                send_sem=side_send.at[d - 1, half, way, step],
+                recv_sem=side_recv.at[d - 1, half, way, step],
+                device_id={"groups": group_at(d)},
+                device_id_type=MESH_ID,
+            )
+            side.start()
+            sides.append(side)
+
+    late = {}
+    for k in range(3):
+        for step in range(steps):
+            for half in range(2):
+                for way in range(2):
+                    if step >= counts[half][way]:
+                        continue
+                    if step:
+                        received(k, half, way, step - 1, late.pop((k, half, way)))
+                    copy = ring_copy(k, half, way, step)
+                    copy.start()
+                    everything.append(copy)
+                    late[(k, half, way)] = copy
+            if step == 0 and k == 0:
+                for copy in own_copies:
+                    copy.start()
+            if step == 0 and k:
+                for half in range(2):
+                    for way in range(2):
+                        received(k - 1, half, way, counts[half][way] - 1, late.pop((k - 1, half, way)))
+        if k == 0:
+            for d, copy in enumerate(x_copies):
+                copy.wait_recv()
+                for c in range(1, cores):
+                    on = pltpu.make_async_remote_copy(
+                        src_ref=arrived.at[d, :, columns],
+                        dst_ref=arrived.at[d, :, columns],
+                        send_sem=core_send.at[d, c - 1],
+                        recv_sem=core_recv.at[d, c - 1],
+                        device_id={"mp": core_at(c)},
+                        device_id_type=MESH_ID,
+                    )
+                    on.start()
+                    core_copies.append(on)
+    for half in range(2):
+        for way in range(2):
+            received(2, half, way, counts[half][way] - 1, late.pop((2, half, way)))
+    for copy in sides + core_copies:
+        copy.wait_recv()
+    for copy in everything + sides + core_copies + x_copies:
+        copy.wait_send()
+    for copy in own_copies:
+        copy.wait()
+
+
+def gathered(sizes, first, out_t, z_own, inputs):
+    groups, seqs, cores = sizes
+    steps = seqs // 2
+    anywhere = pl.BlockSpec(memory_space=pl.ANY)
+    dma = pltpu.SemaphoreType.DMA
+
+    def like(lead, array):
+        return jax.ShapeDtypeStruct(lead + array.shape, array.dtype)
+
+    others, peers = max(groups - 1, 1), max(cores - 1, 1)
+    return pl.pallas_call(
+        functools.partial(gather_kernel, sizes),
+        in_specs=[anywhere] * 4,
+        out_specs=[anywhere] * 4,
+        out_shape=[
+            like((seqs,), first),
+            like((groups, seqs), out_t[0]),
+            like((seqs,), z_own),
+            like((others,), inputs),
+        ],
+        scratch_shapes=[
+            dma((3, 2, 2, steps)),
+            dma((3, 2, 2, steps)),
+            dma((others, 2, 2, steps)),
+            dma((others, 2, 2, steps)),
+            dma((others,)),
+            dma((others,)),
+            dma((others, peers)),
+            dma((others, peers)),
+            dma((2 + groups,)),
+        ],
+        compiler_params=pltpu.CompilerParams(collective_id=0, has_side_effects=True),
+    )(first, out_t, z_own, inputs)
 
 
 def shards(
@@ -108,28 +281,21 @@
         ],
         axis=1,
     )
-    first_all = lax.all_gather(first, "seq", axis=0, tiled=True)
-
-    part = depth // cores
-    own_part = lax.dynamic_slice_in_dim(inputs, core * part, part, 1)
-    batches = [inputs]
-    for d in range(1, groups):
-        arrived = turned(own_part, "groups", d)
-        joined = jnp.zeros((rows, depth), BF16)
-        joined = lax.dynamic_update_slice_in_dim(joined, arrived, core * part, 1)
-        for c in range(1, cores):
-            other = turned(arrived, "mp", c)
-            joined = lax.dynamic_update_slice_in_dim(
-                joined, other, lax.rem(core + cores - c, cores) * part, 1
-            )
-        batches.append(joined)
-    batch = jnp.concatenate(batches, axis=0)
-
-    out_t, first_all = lax.optimization_barrier((mine(out_weight, 0, width).T, first_all))
-    out_all = lax.all_gather(out_t, "seq", axis=0, tiled=True)
-    z_own, out_all = lax.optimization_barrier((mine(zx_weight[:, 0, :], 1, width), out_all))
-    z_all = lax.all_gather(z_own, "seq", axis=0, tiled=True)
-    out_pieces = [out_all] + [turned(out_all, "groups", d) for d in range(1, groups)]
+    out_t = jnp.stack(
+        [
+            lax.dynamic_slice_in_dim(
+                out_weight, lax.rem(group + groups - d, groups) * width, width, 0
+            ).T
+            for d in range(groups)
+        ]
+    )
+    first_all, out_pieces, z_all, arrived = gathered(
+        (groups, seqs, cores), first, out_t, mine(zx_weight[:, 0, :], 1, width), inputs
+    )
+    first_all = first_all.reshape(seqs * slab, first.shape[1])
+    z_all = z_all.reshape(seqs * slab, width)
+    out_pieces = [out_pieces[d].reshape(-1, width) for d in range(groups)]
+    batch = jnp.concatenate([inputs[None], arrived], axis=0).reshape(groups * rows, depth)
 
     summed = jnp.dot(batch, first_all, preferred_element_type=F32)
     raw_x = summed[:, :width].astype(BF16)

time: 365 us -> 263 us (0.72)
  the two profiles are of different devices: /device:TPU:29 before, /device:TPU:0 now
where the time goes in v2:
time: 263 us
  Pallas kernels  121 us (46%)
  other arithmetic  35.3 us (13%)
  local copies, waits for them, and re-layouts  32.3 us (12%)
  starting transfers between devices  25.7 us (10%)
  waiting for transfers between devices  25.7 us (10%)
  matrix products  22.3 us (8%)
    pallas_call x1, Pallas kernels, gathered(): pl.pallas_call(functools.partial(gather_kernel, sizes), in_specs=[anywher...  117 us
    ppermute x5, starting transfers between devices, shifted(): lax.ppermute(block, axis, [(i, i + distance) for i in range(size - distan...  24.8 us
    ppermute x5, waiting for transfers between devices, shifted(): lax.ppermute(block, axis, [(i, i + distance) for i in range(size - distan...  13.7 us
    ppermute x5, waiting for transfers between devices, turned(): lax.ppermute(block, axis, [(i, (i + distance) % size) for i in range(size)])  12 us
    dot_general x1, matrix products, shards(): gate_z = jnp.dot(batch, z_all, preferred_element_type=F32).astype(BF16)  8.29 us
    dot_general x2, matrix products, shards(): lax.dot_general(piece, out_pieces[d], (((1,), (1,)), ((), ())), preferred...  7.75 us
    unnamed x63, local copies, waits for them, and re-layouts  7.74 us
    another operation x2, other arithmetic, shards(): jnp.stack([held[b] + wide(passed[b])[:, :, None] * state for b in range(b...  7.25 us
  transfers between devices with their start and end apart: 10, of which 6 were waited for; matrix products, arithmetic and copies ran while one was open for 11% of the time, Pallas kernels for 1%

profile of v2, /device:TPU:0, one launch (start us, length us, event | category | flops | bytes accessed | tf_op | source)
XLA Modules:
  0.0 262.8 jit_solution(2513530897329928903)
XLA Ops:
  0.9 4.7 %fusion.54 = (bf16[320,1,1280]{2,1,0:T(2,128)(2,1)S(1)}, bf16[320,1,1280]{2,1,0:T(2,128)(2,1)S(1)}) fusion(bf16[320,2,1280]{2,1,0:T(2,128)(2,1)} %param.14), kind=kLoop, calls=%fused_computation.124 | loop fusion | bytes 3276800 | tf_op jit(solution)/shard_map/slice | solution.py:293
  5.6 1.7 constant_dynamic-slice_fusion
  10.6 117.1 %shard_map.127 = (bf16[8,320,896]{2,1,0:T(8,128)(2,1)}, bf16[2,8,320,640]{3,2,1,0:T(8,128)(2,1)}, bf16[8,320,640]{2,1,0:T(8,128)(2,1)}, bf16[1,512,2560]{2,1,0:T(8,128)(2,1)}) custom-call(bf16[320,896]{1,0:T(8,128)(2,1)} %fusion.14.first_ref, bf16[2,320,640]{2,1,0:T(8,128)(2,1)} %pad_maximum_fusion.3.out_ref, bf16[320,640]{1,0:T(8,128)(2,1)} %bitcast.132, ...), custom_call_target="tpu_custom_call" | custom-call | tf_op jit(solution)/shard_map/pallas_call | solution.py:220
  127.7 2.4 pad_maximum_fusion
  130.8 5.1 %fusion.57 = (bf16[1024,896]{0,1:T(8,128)(2,1)S(1)}, f32[1024,896]{0,1:T(8,128)S(1)}) fusion(bf16[1024,2560]{1,0:T(8,128)(2,1)S(1)} %bitcast.125, bf16[2560,896]{1,0:T(8,128)(2,1)S(1)} %bitcast.146), kind=kOutput, calls=%fused_computation.127 | convolution fusion | flops 4698537984 | bytes 15335424 | tf_op jit(solution)/shard_map/dot_general | solution.py:300
  137.6 2.3 reduce-window.6
  140.5 1.4 slice.164
  143.4 3.1 %copy.63 = bf16[1024,896]{1,0:T(8,128)(2,1)S(1)} copy(bf16[1024,896]{0,1:T(8,128)(2,1)} %pad_maximum_fusion.2) | data formatting | bytes 3670016 | tf_op jit(solution)/shard_map/reshape | solution.py:313
  146.5 3.7 %collective-permute-start.1 = (bf16[2,3,896]{2,1,0:T(4,128)(2,1)S(1)}, bf16[2,3,896]{2,1,0:T(4,128)(2,1)S(1)}, u32[]{:S(2)}, u32[]{:S(2)}) collective-permute-start(bf16[2,3,896]{2,1,0:T(4,128)(2,1)S(1)} %slice.166), channel_id=1, source_target_pairs={{0,2},{2,4},{4,6},{6,8},{8,10},{10,12},{12,14},{1,3},{3,5},{5,7},{... | collective-permute-start | bytes 32264 | tf_op jit(solution)/shard_map/ppermute | solution.py:25
  150.5 2.1 copy.50
  152.8 6.2 %multiply_convert_fusion = bf16[2,512,896]{2,1,0:T(8,128)(2,1)S(1)} fusion(bf16[2,512,896]{2,1,0:T(8,128)(2,1)} %bitcast.122, bf16[2,3,896]{2,1,0:T(4,128)(2,1)S(1)} %collective-permute-done.1, f32[896]{0:T(1024)S(1)} %get-tuple-element.17, f32[896]{0:T(1024)S(1)} %get-tuple-element.18, f32[896]{0:T(1024)S(1)} %get-tuple-element.16, ...), kind=kLoop, calls=%fused_computation.2 | loop fusion | flops 23855104 | bytes 3698688 | tf_op jit(solution)/shard_map/convert_element_type | solution.py:320
  160.8 2.9 %fusion.12 = bf16[2,640,128]{2,0,1:T(2,128)(2,1)S(1)} fusion(f32[2,1,640,128]{3,2,1,0:T(8,128)S(1)} %get-tuple-element.42, f32[2,1,640,128]{3,2,1,0:T(8,128)S(1)} %get-tuple-element.43, f32[2,640]{0,1:T(8,128)S(1)} %bitcast_multiply_fusion.1, f32[2,640]{0,1:T(8,128)S(1)} %bitcast.137), kind=kLoop, calls=%fused_computation.32 | loop fusion | flops 655360 | bytes 1648640 | tf_op jit(solution)/shard_map/convert_element_type | solution.py:353
  163.9 3.5 %collective-permute-start.3 = (bf16[2,656,128]{2,0,1:T(2,128)(2,1)S(1)}, bf16[2,656,128]{2,0,1:T(2,128)(2,1)S(1)}, u32[]{:S(2)}, u32[]{:S(2)}) collective-permute-start(bf16[2,656,128]{2,0,1:T(2,128)(2,1)S(1)} %fusion.16), channel_id=1, source_target_pairs={{0,4},{2,6},{4,8},{6,10},{8,12},{10,14},{1,5},{3,7},{5,9},{7,11},{... | collective-permute-start | bytes 1007624 | tf_op jit(solution)/shard_map/ppermute | solution.py:25
  167.5 2.8 %collective-permute-start.2 = (bf16[2,656,128]{2,0,1:T(2,128)(2,1)S(1)}, bf16[2,656,128]{2,0,1:T(2,128)(2,1)S(1)}, u32[]{:S(2)}, u32[]{:S(2)}) collective-permute-start(bf16[2,656,128]{2,0,1:T(2,128)(2,1)S(1)} %fusion.16), channel_id=1, source_target_pairs={{0,2},{2,4},{4,6},{6,8},{8,10},{10,12},{12,14},{1,3},{3,5},{5,7},{... | collective-permute-start | bytes 1007624 | tf_op jit(solution)/shard_map/ppermute | solution.py:25
  170.3 4.7 %collective-permute-done.3 = bf16[2,656,128]{2,0,1:T(2,128)(2,1)S(1)} collective-permute-done((bf16[2,656,128]{2,0,1:T(2,128)(2,1)S(1)}, bf16[2,656,128]{2,0,1:T(2,128)(2,1)S(1)}, u32[]{:S(2)}, u32[]{:S(2)}) %collective-permute-start.3) | collective-permute-done | bytes 335904 | tf_op jit(solution)/shard_map/ppermute | solution.py:25
  174.9 2.4 collective-permute-done.2
  178.8 9.4 %collective-permute-start.4 = (bf16[2,656,128]{2,0,1:T(2,128)(2,1)S(1)}, bf16[2,656,128]{2,0,1:T(2,128)(2,1)S(1)}, u32[]{:S(2)}, u32[]{:S(2)}) collective-permute-start(bf16[2,656,128]{2,0,1:T(2,128)(2,1)S(1)} %pad_maximum_fusion.5), channel_id=1, source_target_pairs={{0,4},{2,6},{4,8},{6,10},{8,12},{10,14},{1,5},{3,7},{5,9},{7,11},{... | collective-permute-start | bytes 1007624 | tf_op jit(solution)/shard_map/ppermute | solution.py:25
  188.2 6.6 %collective-permute-done.4 = bf16[2,656,128]{2,0,1:T(2,128)(2,1)S(1)} collective-permute-done((bf16[2,656,128]{2,0,1:T(2,128)(2,1)S(1)}, bf16[2,656,128]{2,0,1:T(2,128)(2,1)S(1)}, u32[]{:S(2)}, u32[]{:S(2)}) %collective-permute-start.4) | collective-permute-done | bytes 335904 | tf_op jit(solution)/shard_map/ppermute | solution.py:25
  195.0 2.6 fusion.48
  198.7 5.4 %collective-permute-start.5 = (bf16[2,656,128]{2,0,1:T(2,128)(2,1)}, bf16[2,656,128]{2,0,1:T(2,128)(2,1)}, u32[]{:S(2)}, u32[]{:S(2)}) collective-permute-start(bf16[2,656,128]{2,0,1:T(2,128)(2,1)} %pad_maximum_fusion.6), channel_id=1, source_target_pairs={{0,8},{2,10},{4,12},{6,14},{1,9},{3,11},{5,13},{7,15},{16,24},{18,... | collective-permute-start | bytes 1007624 | tf_op jit(solution)/shard_map/ppermute | solution.py:25
  204.1 8.3 %fusion.6 = f32[1024,640]{1,0:T(8,128)} fusion(bf16[1024,2560]{1,0:T(8,128)(2,1)} %bitcast.126, bf16[2560,640]{1,0:T(8,128)(2,1)S(1)} %bitcast.147), kind=kOutput, calls=%fused_computation.20 | convolution fusion | flops 3356753920 | bytes 11141120 | tf_op jit(solution)/shard_map/dot_general | solution.py:376
  213.0 1.7 broadcast_in_dim.41
  214.7 3.2 %copy.59 = f32[4,256,640]{2,1,0:T(8,128)} copy(f32[4,256,640]{1,2,0:T(8,128)} %bitcast.117) | data formatting | bytes 5242880 | tf_op jit(solution)/shard_map/reshape | solution.py:334
  218.1 3.6 %shard_map.128 = f32[4,256,640]{2,1,0:T(8,128)S(1)} custom-call(bf16[4,256,640]{2,1,0:T(8,128)(2,1)S(1)} %slice.175.values_ref, bf16[4,256,128]{2,1,0:T(8,128)(2,1)S(1)} %get-tuple-element.35.keys_ref, bf16[4,256,128]{2,1,0:T(8,128)(2,1)S(1)} %get-tuple-element.34.queries_ref, f32[4,256,10]{2,1,0:T(8,128)S(1)} %copy.46.cum_ref, ...), custom_call_target="tpu_custom_call" | custom-call | flops 402653184 | bytes 3932160 | tf_op jit(solution)/shard_map/pallas_call | solution.py:53
  221.9 6.3 %convert_bitcast_fusion = (bf16[2,1,640,128]{3,0,2,1:T(2,128)(2,1)S(1)}, bf16[2,1,640,128]{3,0,2,1:T(2,128)(2,1)S(1)}) fusion(f32[2,640,128]{2,0,1:T(2,128)} %get-tuple-element.24, bf16[2,656,128]{2,0,1:T(2,128)(2,1)} %collective-permute-done.5, f32[2,640]{0,1:T(8,128)S(1)} %bitcast.134, f32[2,640]{0,1:T(8,128)S(1)} %bitcast.135, ...), kind=kLoop, calls=%fused_computation.48 | loop fusion | flops 1310720 | bytes 2309120 | tf_op jit(solution)/shard_map/stack | solution.py:378
  234.5 2.3 fusion.51
  236.8 4.4 %fusion.10 = f32[512,2560]{1,0:T(8,128)S(1)} fusion(bf16[2560,640]{1,0:T(8,128)(2,1)} %bitcast.128, bf16[2,512,640]{2,1,0:T(8,128)(2,1)} %copy-done.13), kind=kOutput, calls=%fused_computation.28 | convolution fusion | flops 1677721600 | bytes 9175040 | tf_op jit(solution)/shard_map/dot_general | solution.py:399
  241.1 7.6 %collective-permute-done.6 = bf16[512,640]{1,0:T(8,128)(2,1)} collective-permute-done((bf16[512,640]{1,0:T(8,128)(2,1)}, bf16[512,640]{1,0:T(8,128)(2,1)}, u32[]{:S(2)}, u32[]{:S(2)}) %collective-permute-start.6) | collective-permute-done | bytes 655392 | tf_op jit(solution)/shard_map/ppermute | solution.py:20
  248.8 3.4 %convolution_add_fusion = f32[512,2560]{1,0:T(8,128)S(1)} fusion(f32[512,2560]{1,0:T(8,128)S(1)} %fusion.10, bf16[512,640]{1,0:T(8,128)(2,1)} %collective-permute-done.6, bf16[2560,640]{1,0:T(8,128)(2,1)S(1)} %bitcast.114), kind=kOutput, calls=%fused_computation.1 | convolution fusion | flops 1679032320 | bytes 14417920 | tf_op jit(solution)/shard_map/dot_general | solution.py:399
  252.2 2.3 copy-done.2
  255.2 3.2 %collective-permute-done.8 = f32[512]{0:T(512)S(1)} collective-permute-done((f32[512]{0:T(512)S(1)}, f32[512]{0:T(512)S(1)}, u32[]{:S(2)}, u32[]{:S(2)}) %collective-permute-start.8) | collective-permute-done | bytes 2080 | tf_op jit(solution)/shard_map/ppermute | solution.py:20
  259.6 3.2 %multiply_convert_fusion.1 = bf16[512,1280]{1,0:T(8,128)(2,1)} fusion(bf16[512,1280]{1,0:T(8,128)(2,1)S(1)} %collective-permute-done.7, f32[512,2560]{1,0:T(8,128)} %copy-done.2, s32[]{:T(128)S(6)} %select_n.43, f32[512]{0:T(512)S(1)} %add_rsqrt_fusion), kind=kLoop, calls=%fused_computation.10 | loop fusion | flops 2621440 | bytes 5244932 | tf_op jit(solution)/shard_map/convert_element_type | solution.py:413
  (145 shorter events, 22.6 us)
Async XLA Ops:
  0.0 8.2 %copy-start = (bf16[320,256]{1,0:T(8,128)(2,1)S(1)}, bf16[320,256]{1,0:T(8,128)(2,1)}, u32[]{:S(2)}) copy-start(bf16[320,256]{1,0:T(8,128)(2,1)} %param.15) | copy-start | bytes 491524
  9.7 118.0 %copy-start.5 = (bf16[512,2560]{1,0:T(8,128)(2,1)S(1)}, bf16[512,2560]{1,0:T(8,128)(2,1)}, u32[]{:S(2)}) copy-start(bf16[512,2560]{1,0:T(8,128)(2,1)} %x_ref.1) | copy-start | bytes 7864324
  127.7 3.1 %copy-start.21 = (bf16[8,320,896]{2,1,0:T(8,128)(2,1)S(1)}, bf16[8,320,896]{2,1,0:T(8,128)(2,1)}, u32[]{:S(2)}) copy-start(bf16[8,320,896]{2,1,0:T(8,128)(2,1)} %get-tuple-element.10) | copy-start | bytes 13762564
  130.1 5.8 %copy-start.11 = (bf16[2,512,2560]{2,1,0:T(8,128)(2,1)}, bf16[2,512,2560]{2,1,0:T(8,128)(2,1)S(1)}, u32[]{:S(2)}) copy-start(bf16[2,512,2560]{2,1,0:T(8,128)(2,1)S(1)} %pad_maximum_fusion) | copy-start | bytes 15728644
  130.8 6.3 %copy-start.16 = (f32[4,1280]{1,0:T(4,128)S(1)}, f32[4,1280]{1,0:T(4,128)}, u32[]{:S(2)}) copy-start(f32[4,1280]{1,0:T(4,128)} %param.17) | copy-start | bytes 61444
  130.8 6.4 %copy-start.18 = (f32[1280]{0:T(1024)S(1)}, f32[1280]{0:T(1024)}, u32[]{:S(2)}) copy-start(f32[1280]{0:T(1024)} %param.18) | copy-start | bytes 15364
  130.8 6.4 %copy-start.23 = (f32[20]{0:T(128)S(1)}, f32[20]{0:T(128)}, u32[]{:S(2)}) copy-start(f32[20]{0:T(128)} %param.22) | copy-start | bytes 244
  130.8 6.5 %copy-start.24 = (f32[20]{0:T(128)S(1)}, f32[20]{0:T(128)}, u32[]{:S(2)}) copy-start(f32[20]{0:T(128)} %param.21) | copy-start | bytes 244
  130.8 9.7 %copy-start.20 = (f32[256]{0:T(256)S(1)}, f32[256]{0:T(256)}, u32[]{:S(2)}) copy-start(f32[256]{0:T(256)} %param.20) | copy-start | bytes 3076
  137.1 4.9 %collective-permute-start = (bf16[1024,128]{0,1:T(8,128)(2,1)S(1)}, bf16[1024,128]{0,1:T(8,128)(2,1)S(1)}, u32[]{:S(2)}, u32[]{:S(2)}) collective-permute-start(bf16[1024,128]{0,1:T(8,128)(2,1)S(1)} %get-tuple-element.36), channel_id=1, source_target_pairs={{0,1},{1,0},{2,3},{3,2},{4,5},{5,4},{6,7},{7,6},{8,9},{9,8},{10,11... | collective-permute-start | bytes 786440 | tf_op jit(solution)/shard_map/ppermute | solution.py:20
  146.5 3.7 %copy-start.9 = (bf16[1024,896]{1,0:T(8,128)(2,1)}, bf16[1024,896]{1,0:T(8,128)(2,1)S(1)}, u32[]{:S(2)}) copy-start(bf16[1024,896]{1,0:T(8,128)(2,1)S(1)} %copy.63) | copy-start | bytes 5505028
  146.5 6.3 %collective-permute-start.1 = (bf16[2,3,896]{2,1,0:T(4,128)(2,1)S(1)}, bf16[2,3,896]{2,1,0:T(4,128)(2,1)S(1)}, u32[]{:S(2)}, u32[]{:S(2)}) collective-permute-start(bf16[2,3,896]{2,1,0:T(4,128)(2,1)S(1)} %slice.166), channel_id=1, source_target_pairs={{0,2},{2,4},{4,6},{6,8},{8,10},{10,12},{12,14},{1,3},{3,5},{5,7},{... | collective-permute-start | bytes 32264 | tf_op jit(solution)/shard_map/ppermute | solution.py:25
  150.4 2.3 copy-start.17
  152.7 7.3 %copy-start.12 = (f32[2,640]{0,1:T(8,128)}, f32[2,640]{0,1:T(8,128)S(1)}, u32[]{:S(2)}) copy-start(f32[2,640]{0,1:T(8,128)S(1)} %bitcast_multiply_fusion.1) | copy-start | bytes 15364
  152.8 6.3 %copy-start.6 = (f32[4,256,640]{2,1,0:T(8,128)S(1)}, f32[4,256,640]{2,1,0:T(8,128)}, u32[]{:S(2)}) copy-start(f32[4,256,640]{2,1,0:T(8,128)} %copy.50) | copy-start | bytes 7864324
  159.1 58.9 %copy-start.3 = (bf16[2,512,896]{2,1,0:T(8,128)(2,1)}, bf16[2,512,896]{2,1,0:T(8,128)(2,1)S(1)}, u32[]{:S(2)}) copy-start(bf16[2,512,896]{2,1,0:T(8,128)(2,1)S(1)} %multiply_convert_fusion) | copy-start | bytes 5505028
  163.9 11.0 %collective-permute-start.3 = (bf16[2,656,128]{2,0,1:T(2,128)(2,1)S(1)}, bf16[2,656,128]{2,0,1:T(2,128)(2,1)S(1)}, u32[]{:S(2)}, u32[]{:S(2)}) collective-permute-start(bf16[2,656,128]{2,0,1:T(2,128)(2,1)S(1)} %fusion.16), channel_id=1, source_target_pairs={{0,4},{2,6},{4,8},{6,10},{8,12},{10,14},{1,5},{3,7},{5,9},{7,11},{... | collective-permute-start | bytes 1007624 | tf_op jit(solution)/shard_map/ppermute | solution.py:25
  167.5 9.9 %collective-permute-start.2 = (bf16[2,656,128]{2,0,1:T(2,128)(2,1)S(1)}, bf16[2,656,128]{2,0,1:T(2,128)(2,1)S(1)}, u32[]{:S(2)}, u32[]{:S(2)}) collective-permute-start(bf16[2,656,128]{2,0,1:T(2,128)(2,1)S(1)} %fusion.16), channel_id=1, source_target_pairs={{0,2},{2,4},{4,6},{6,8},{8,10},{10,12},{12,14},{1,3},{3,5},{5,7},{... | collective-permute-start | bytes 1007624 | tf_op jit(solution)/shard_map/ppermute | solution.py:25
  178.8 16.0 %collective-permute-start.4 = (bf16[2,656,128]{2,0,1:T(2,128)(2,1)S(1)}, bf16[2,656,128]{2,0,1:T(2,128)(2,1)S(1)}, u32[]{:S(2)}, u32[]{:S(2)}) collective-permute-start(bf16[2,656,128]{2,0,1:T(2,128)(2,1)S(1)} %pad_maximum_fusion.5), channel_id=1, source_target_pairs={{0,4},{2,6},{4,8},{6,10},{8,12},{10,14},{1,5},{3,7},{5,9},{7,11},{... | collective-permute-start | bytes 1007624 | tf_op jit(solution)/shard_map/ppermute | solution.py:25
  194.9 9.2 %copy-start.22 = (bf16[8,320,640]{2,1,0:T(8,128)(2,1)S(1)}, bf16[8,320,640]{2,1,0:T(8,128)(2,1)}, u32[]{:S(2)}) copy-start(bf16[8,320,640]{2,1,0:T(8,128)(2,1)} %get-tuple-element.11) | copy-start | bytes 9830404
  198.7 23.1 %collective-permute-start.5 = (bf16[2,656,128]{2,0,1:T(2,128)(2,1)}, bf16[2,656,128]{2,0,1:T(2,128)(2,1)}, u32[]{:S(2)}, u32[]{:S(2)}) collective-permute-start(bf16[2,656,128]{2,0,1:T(2,128)(2,1)} %pad_maximum_fusion.6), channel_id=1, source_target_pairs={{0,8},{2,10},{4,12},{6,14},{1,9},{3,11},{5,13},{7,15},{16,24},{18,... | collective-permute-start | bytes 1007624 | tf_op jit(solution)/shard_map/ppermute | solution.py:25
  204.1 8.5 %copy-start.19 = (f32[1280]{0:T(1024)S(1)}, f32[1280]{0:T(1024)}, u32[]{:S(2)}) copy-start(f32[1280]{0:T(1024)} %param.24) | copy-start | bytes 15364
  204.1 8.6 %copy-start.25 = (f32[20]{0:T(128)S(1)}, f32[20]{0:T(128)}, u32[]{:S(2)}) copy-start(f32[20]{0:T(128)} %param.23) | copy-start | bytes 244
  221.9 7.4 %copy-start.4 = (bf16[2,512,896]{2,1,0:T(8,128)(2,1)S(1)}, bf16[2,512,896]{2,1,0:T(8,128)(2,1)}, u32[]{:S(2)}) copy-start(bf16[2,512,896]{2,1,0:T(8,128)(2,1)} %copy-done.3) | copy-start | bytes 5505028
  229.3 5.2 %slice-start = ((s8[6553600]{0:T(1024)(128)(4,1)}), s8[4194304]{0:T(1024)(128)(4,1)S(1)}, s32[]{:S(2)}) async-start(s8[6553600]{0:T(1024)(128)(4,1)} %bitcast.123), calls=%async_computation | async-start | bytes 8388608
  231.1 3.4 %slice-start.1 = ((s8[6553600]{0:T(1024)(128)(4,1)}), s8[2359296]{0:T(1024)(128)(4,1)S(1)}, s32[]{:S(2)}) async-start(s8[6553600]{0:T(1024)(128)(4,1)} %bitcast.123), calls=%async_computation.1 | async-start | bytes 4718592
  234.0 14.7 %collective-permute-start.6 = (bf16[512,640]{1,0:T(8,128)(2,1)}, bf16[512,640]{1,0:T(8,128)(2,1)}, u32[]{:S(2)}, u32[]{:S(2)}) collective-permute-start(bf16[512,640]{1,0:T(8,128)(2,1)} %slice_bitcast_fusion), channel_id=1, source_target_pairs={{0,16},{16,0},{1,17},{17,1},{2,18},{18,2},{3,19},{19,3},{4,20},{20... | collective-permute-start | bytes 1966088 | tf_op jit(solution)/shard_map/ppermute | solution.py:20
  252.2 2.3 copy-start.2
  254.7 4.9 %collective-permute-start.7 = (bf16[512,1280]{1,0:T(8,128)(2,1)S(1)}, bf16[512,1280]{1,0:T(8,128)(2,1)S(1)}, u32[]{:S(2)}, u32[]{:S(2)}) collective-permute-start(bf16[512,1280]{1,0:T(8,128)(2,1)S(1)} %dynamic-slice_convert_fusion), channel_id=1, source_target_pairs={{0,1},{1,0},{2,3},{3,2},{4,5},{5,4},{6,7},{7,6},{8,9},{9,8},{10,11... | collective-permute-start | bytes 3932168 | tf_op jit(solution)/shard_map/ppermute | solution.py:20
  254.8 3.7 %collective-permute-start.8 = (f32[512]{0:T(512)S(1)}, f32[512]{0:T(512)S(1)}, u32[]{:S(2)}, u32[]{:S(2)}) collective-permute-start(f32[512]{0:T(512)S(1)} %bitcast.145), channel_id=1, source_target_pairs={{0,16},{16,0},{1,17},{17,1},{2,18},{18,2},{3,19},{19,3},{4,20},{20... | collective-permute-start | bytes 6152 | tf_op jit(solution)/shard_map/ppermute | solution.py:20
  258.4 1.2 collective-permute-start.9
  259.6 3.2 %copy-start.1 = (bf16[320,256]{1,0:T(8,128)(2,1)S(1)}, bf16[320,256]{1,0:T(8,128)(2,1)}, u32[]{:S(2)}) copy-start(bf16[320,256]{1,0:T(8,128)(2,1)} %param.15) | copy-start | bytes 491524
  (6 other events, 8.5 us)

commit v3 on v2

--- a/solution.py
+++ b/solution.py
@@ -73,7 +73,7 @@
 MESH_ID = pl.DeviceIdType.MESH
 
 
-def gather_kernel(sizes, first_ref, out_ref, z_ref, x_ref, first_all, out_all, z_all, arrived, *sems):
+def gather_kernel(sizes, first_ref, out_ref, x_ref, first_all, out_all, arrived, *sems):
     groups, seqs, cores = sizes
     ring_send, ring_recv, side_send, side_recv, x_send, x_recv, core_send, core_recv, own_sem = sems
     group, seq, core = (lax.axis_index(a) for a in ("groups", "seq", "mp"))
@@ -117,9 +117,9 @@
     for copy in x_copies:
         copy.start()
 
-    owns = [first_ref, out_ref.at[0], z_ref]
-    alls = [first_all, out_all.at[0], z_all]
-    locals_ = [(first_ref, first_all.at[seq]), (z_ref, z_all.at[seq])]
+    owns = [first_ref, out_ref.at[0]]
+    alls = [first_all, out_all.at[0]]
+    locals_ = [(first_ref, first_all.at[seq])]
     locals_ += [(out_ref.at[d], out_all.at[d, seq]) for d in range(groups)]
     own_copies = [
         pltpu.make_async_copy(source, target, own_sem.at[i])
@@ -163,7 +163,7 @@
             sides.append(side)
 
     late = {}
-    for k in range(3):
+    for k in range(2):
         for step in range(steps):
             for half in range(2):
                 for way in range(2):
@@ -198,7 +198,7 @@
                     core_copies.append(on)
     for half in range(2):
         for way in range(2):
-            received(2, half, way, counts[half][way] - 1, late.pop((2, half, way)))
+            received(1, half, way, counts[half][way] - 1, late.pop((1, half, way)))
     for copy in sides + core_copies:
         copy.wait_recv()
     for copy in everything + sides + core_copies + x_copies:
@@ -207,7 +207,7 @@
         copy.wait()
 
 
-def gathered(sizes, first, out_t, z_own, inputs):
+def gathered(sizes, first, out_t, inputs):
     groups, seqs, cores = sizes
     steps = seqs // 2
     anywhere = pl.BlockSpec(memory_space=pl.ANY)
@@ -219,27 +219,27 @@
     others, peers = max(groups - 1, 1), max(cores - 1, 1)
     return pl.pallas_call(
         functools.partial(gather_kernel, sizes),
-        in_specs=[anywhere] * 4,
-        out_specs=[anywhere] * 4,
+        in_specs=[anywhere] * 3,
+        out_specs=[anywhere] * 3,
         out_shape=[
             like((seqs,), first),
             like((groups, seqs), out_t[0]),
-            like((seqs,), z_own),
             like((others,), inputs),
         ],
         scratch_shapes=[
-            dma((3, 2, 2, steps)),
-            dma((3, 2, 2, steps)),
+            dma((2, 2, 2, steps)),
+            dma((2, 2, 2, steps)),
             dma((others, 2, 2, steps)),
             dma((others, 2, 2, steps)),
             dma((others,)),
             dma((others,)),
             dma((others, peers)),
             dma((others, peers)),
-            dma((2 + groups,)),
+            dma((1 + groups,)),
         ],
         compiler_params=pltpu.CompilerParams(collective_id=0, has_side_effects=True),
-    )(first, out_t, z_own, inputs)
+        cost_estimate=pl.CostEstimate(flops=0, bytes_accessed=200 * 2**20, transcendentals=0),
+    )(first, out_t, inputs)
 
 
 def shards(
@@ -289,11 +289,9 @@
             for d in range(groups)
         ]
     )
-    first_all, out_pieces, z_all, arrived = gathered(
-        (groups, seqs, cores), first, out_t, mine(zx_weight[:, 0, :], 1, width), inputs
-    )
+    z_all = lax.all_gather(mine(zx_weight[:, 0, :], 1, width), "seq", axis=0, tiled=True)
+    first_all, out_pieces, arrived = gathered((groups, seqs, cores), first, out_t, inputs)
     first_all = first_all.reshape(seqs * slab, first.shape[1])
-    z_all = z_all.reshape(seqs * slab, width)
     out_pieces = [out_pieces[d].reshape(-1, width) for d in range(groups)]
     batch = jnp.concatenate([inputs[None], arrived], axis=0).reshape(groups * rows, depth)
 
@@ -356,24 +354,27 @@
         decay = message[:, width, :heads].astype(F32) + message[:, width + 1, :heads].astype(F32)
         return message[:, :width].astype(F32), decay
 
+    inner = inner_blocks(
+        values, keys_b, queries_c, cum, (jnp.log(steps_dt) - cum).transpose(0, 2, 1)
+    )
+    gate_z = jnp.dot(batch, z_all, preferred_element_type=F32).astype(BF16)
     message = packed(held[-1], passed[-1])
-    state, decay = unpacked(shifted(message, "seq", 1))
+    near, far = shifted(message, "seq", 1), shifted(message, "seq", 2)
+    near, far, inner = lax.optimization_barrier((near, far, inner))
+    state, decay = unpacked(near)
     if seqs > 2:
-        far_state, far_decay = unpacked(shifted(message, "seq", 2))
+        far_state, far_decay = unpacked(far)
         state = state + wide(decay)[:, :, None] * far_state
         decay = decay * far_decay
     reach = 2
     while reach < seqs - 1:
-        far_state, far_decay = unpacked(shifted(packed(state, decay), "seq", reach))
+        far = shifted(packed(state, decay), "seq", reach)
+        if reach == 2:
+            far, gate_z = lax.optimization_barrier((far, gate_z))
+        far_state, far_decay = unpacked(far)
         state = state + wide(decay)[:, :, None] * far_state
         decay = decay * far_decay
         reach *= 2
-
-    inner = inner_blocks(
-        values, keys_b, queries_c, cum, (jnp.log(steps_dt) - cum).transpose(0, 2, 1)
-    )
-
-    gate_z = jnp.dot(batch, z_all, preferred_element_type=F32).astype(BF16)
 
     state_in = jnp.stack(
         [held[b] + wide(passed[b])[:, :, None] * state for b in range(blocks)], axis=1

time: 263 us -> 312 us (1.19)
  the two profiles are of different devices: /device:TPU:0 before, /device:TPU:29 now
where the time goes in v3:
time: 312 us
  Pallas kernels  152 us (49%)
  other arithmetic  42.2 us (14%)
  waiting for transfers between devices  35.9 us (12%)
  local copies, waits for them, and re-layouts  30.5 us (10%)
  matrix products  22.8 us (7%)
  starting transfers between devices  14.5 us (5%)
  between operations  14.2 us (5%)
    pallas_call x1, Pallas kernels, gathered(): pl.pallas_call(functools.partial(gather_kernel, sizes), in_specs=[anywher...  148 us
    ppermute x5, waiting for transfers between devices, shifted(): lax.ppermute(block, axis, [(i, i + distance) for i in range(size - distan...  25.6 us
    ppermute x5, waiting for transfers between devices, turned(): lax.ppermute(block, axis, [(i, (i + distance) % size) for i in range(size)])  10.3 us
    convert_element_type x3, other arithmetic, packed(): return jnp.concatenate([state.astype(BF16), extra], axis=1)  8.89 us
    dot_general x1, matrix products, shards(): gate_z = jnp.dot(batch, z_all, preferred_element_type=F32).astype(BF16)  8.77 us
    dot_general x2, matrix products, shards(): lax.dot_general(piece, out_pieces[d], (((1,), (1,)), ((), ())), preferred...  7.76 us
    ppermute x5, starting transfers between devices, turned(): lax.ppermute(block, axis, [(i, (i + distance) % size) for i in range(size)])  7.68 us
    another operation x2, other arithmetic, shards(): jnp.stack([held[b] + wide(passed[b])[:, :, None] * state for b in range(b...  7.14 us
  transfers between devices with their start and end apart: 11, of which 7 were waited for; matrix products, arithmetic and copies ran while one was open for 19% of the time, Pallas kernels for 49%

profile of v3, /device:TPU:29, one launch (start us, length us, event | category | flops | bytes accessed | tf_op | source)
XLA Modules:
  0.0 311.7 jit_solution(4591688490803942730)
XLA Ops:
  6.5 4.7 %fusion.58 = (bf16[320,1,1280]{2,1,0:T(2,128)(2,1)S(1)}, bf16[320,1,1280]{2,1,0:T(2,128)(2,1)S(1)}) fusion(bf16[320,2,1280]{2,1,0:T(2,128)(2,1)} %param.14), kind=kLoop, calls=%fused_computation.124 | loop fusion | bytes 3276800 | tf_op jit(solution)/shard_map/slice | solution.py:292
  16.1 148.1 %shard_map.127 = (bf16[8,320,896]{2,1,0:T(8,128)(2,1)}, bf16[2,8,320,640]{3,2,1,0:T(8,128)(2,1)}, bf16[1,512,2560]{2,1,0:T(8,128)(2,1)}) custom-call(bf16[320,896]{1,0:T(8,128)(2,1)} %fusion.18.first_ref, bf16[2,320,640]{2,1,0:T(8,128)(2,1)} %pad_maximum_fusion.3.out_ref, bf16[512,2560]{1,0:T(8,128)(2,1)} %x_ref.1), custom_call_target="tpu_custom_call" | custom-call | bytes 209715200 | tf_op jit(solution)/shard_map/pallas_call | solution.py:220
  164.2 2.4 pad_maximum_fusion
  167.3 5.1 %fusion.61 = (bf16[1024,896]{0,1:T(8,128)(2,1)S(1)}, f32[1024,896]{0,1:T(8,128)S(1)}) fusion(bf16[1024,2560]{1,0:T(8,128)(2,1)S(1)} %bitcast.125, bf16[2560,896]{1,0:T(8,128)(2,1)S(1)} %bitcast.145), kind=kOutput, calls=%fused_computation.127 | convolution fusion | flops 4698537984 | bytes 15335424 | tf_op jit(solution)/shard_map/dot_general | solution.py:298
  173.7 2.7 collective-permute-start
  176.8 2.3 reduce-window.6
  182.7 3.1 copy.63
  185.8 1.5 collective-permute-start.1
  187.5 2.1 copy.47
  190.0 2.8 collective-permute-done.1
  192.7 6.3 %multiply_convert_fusion = bf16[2,512,896]{2,1,0:T(8,128)(2,1)S(1)} fusion(bf16[2,512,896]{2,1,0:T(8,128)(2,1)} %bitcast.122, bf16[2,3,896]{2,1,0:T(4,128)(2,1)S(1)} %collective-permute-done.1, f32[896]{0:T(1024)S(1)} %get-tuple-element.25, f32[896]{0:T(1024)S(1)} %get-tuple-element.26, f32[896]{0:T(1024)S(1)} %get-tuple-element.24, ...), kind=kLoop, calls=%fused_computation.2 | loop fusion | flops 23855104 | bytes 3698688 | tf_op jit(solution)/shard_map/convert_element_type | solution.py:318
  199.9 2.9 fusion.16
  206.9 3.6 %shard_map.128 = f32[4,256,640]{2,1,0:T(8,128)S(1)} custom-call(bf16[4,256,640]{2,1,0:T(8,128)(2,1)S(1)} %slice.181.values_ref, bf16[4,256,128]{2,1,0:T(8,128)(2,1)S(1)} %get-tuple-element.43.keys_ref, bf16[4,256,128]{2,1,0:T(8,128)(2,1)S(1)} %get-tuple-element.42.queries_ref, f32[4,256,10]{2,1,0:T(8,128)S(1)} %copy.53.cum_ref, ...), custom_call_target="tpu_custom_call" | custom-call | flops 402653184 | bytes 3932160 | tf_op jit(solution)/shard_map/pallas_call | solution.py:53
  210.5 5.0 %collective-permute-done.2 = bf16[2,656,128]{2,0,1:T(2,128)(2,1)} collective-permute-done((bf16[2,656,128]{2,0,1:T(2,128)(2,1)}, bf16[2,656,128]{2,0,1:T(2,128)(2,1)}, u32[]{:S(2)}, u32[]{:S(2)}) %collective-permute-start.2) | collective-permute-done | bytes 335904 | tf_op jit(solution)/shard_map/ppermute | solution.py:25
  215.5 8.1 %collective-permute-done.3 = bf16[2,656,128]{2,0,1:T(2,128)(2,1)} collective-permute-done((bf16[2,656,128]{2,0,1:T(2,128)(2,1)}, bf16[2,656,128]{2,0,1:T(2,128)(2,1)}, u32[]{:S(2)}, u32[]{:S(2)}) %collective-permute-start.3) | collective-permute-done | bytes 335904 | tf_op jit(solution)/shard_map/ppermute | solution.py:25
  224.4 1.8 fusion.19
  228.0 8.8 %fusion.8 = bf16[1024,640]{1,0:T(8,128)(2,1)} fusion(bf16[1024,2560]{1,0:T(8,128)(2,1)} %bitcast.126, bf16[2560,1,640]{2,0,1:T(8,128)(2,1)} %all-gather.3.cloned.1.call-done), kind=kOutput, calls=%fused_computation.21 | convolution fusion | flops 3356098560 | bytes 9830400 | tf_op jit(solution)/shard_map/dot_general | solution.py:360
  238.3 4.1 %fusion.52 = (bf16[2,640,128]{2,0,1:T(2,128)(2,1)S(1)}, f32[2,640,128]{2,0,1:T(2,128)}) fusion(bf16[2,656,128]{2,0,1:T(2,128)(2,1)} %collective-permute-done.4, f32[2,640]{0,1:T(8,128)S(1)} %bitcast.135, bf16[2,656,128]{2,0,1:T(2,128)(2,1)} %collective-permute-done.3, f32[2,640]{0,1:T(8,128)S(1)} %bitcast.130, bf16[2,656,128]{2,0,1:T(2,128)(2,1)} %collective-permute-done.2), kind=kLoop, calls=%fused_computation.120 | loop fusion | flops 1310720 | bytes 1976320 | tf_op jit(solution)/shard_map/convert_element_type | solution.py:351
  243.6 1.5 collective-permute-start.5
  245.1 1.7 broadcast_in_dim.45
  246.8 3.3 %copy.59 = f32[4,256,640]{2,1,0:T(8,128)} copy(f32[4,256,640]{1,2,0:T(8,128)} %bitcast.119) | data formatting | bytes 5242880 | tf_op jit(solution)/shard_map/reshape | solution.py:332
  250.5 1.6 convert_element_type.187
  252.1 9.8 %collective-permute-done.5 = bf16[2,656,128]{2,0,1:T(2,128)(2,1)} collective-permute-done((bf16[2,656,128]{2,0,1:T(2,128)(2,1)}, bf16[2,656,128]{2,0,1:T(2,128)(2,1)}, u32[]{:S(2)}, u32[]{:S(2)}) %collective-permute-start.5) | collective-permute-done | bytes 335904 | tf_op jit(solution)/shard_map/ppermute | solution.py:25
  261.9 6.2 %convert_bitcast_fusion = (bf16[2,1,640,128]{3,0,2,1:T(2,128)(2,1)S(1)}, bf16[2,1,640,128]{3,0,2,1:T(2,128)(2,1)S(1)}) fusion(f32[2,640,128]{2,0,1:T(2,128)S(1)} %copy-done.15, bf16[2,656,128]{2,0,1:T(2,128)(2,1)} %collective-permute-done.5, f32[2,640]{0,1:T(8,128)S(1)} %bitcast.133, f32[2,640]{0,1:T(8,128)S(1)} %bitcast.134, ...), kind=kLoop, calls=%fused_computation.48 | loop fusion | flops 1310720 | bytes 2309120 | tf_op jit(solution)/shard_map/stack | solution.py:379
  274.1 2.3 fusion.55
  276.3 4.4 %fusion.14 = f32[512,2560]{1,0:T(8,128)S(1)} fusion(bf16[2560,640]{1,0:T(8,128)(2,1)} %bitcast.128, bf16[2,512,640]{2,1,0:T(8,128)(2,1)} %copy-done.14), kind=kOutput, calls=%fused_computation.29 | convolution fusion | flops 1677721600 | bytes 9175040 | tf_op jit(solution)/shard_map/dot_general | solution.py:400
  280.7 7.2 %collective-permute-done.6 = bf16[512,640]{1,0:T(8,128)(2,1)} collective-permute-done((bf16[512,640]{1,0:T(8,128)(2,1)}, bf16[512,640]{1,0:T(8,128)(2,1)}, u32[]{:S(2)}, u32[]{:S(2)}) %collective-permute-start.6) | collective-permute-done | bytes 655392 | tf_op jit(solution)/shard_map/ppermute | solution.py:20
  287.9 3.4 %convolution_add_fusion = f32[512,2560]{1,0:T(8,128)S(1)} fusion(f32[512,2560]{1,0:T(8,128)S(1)} %fusion.14, bf16[512,640]{1,0:T(8,128)(2,1)} %collective-permute-done.6, bf16[2560,640]{1,0:T(8,128)(2,1)S(1)} %bitcast.116), kind=kOutput, calls=%fused_computation.1 | convolution fusion | flops 1679032320 | bytes 14417920 | tf_op jit(solution)/shard_map/dot_general | solution.py:400
  291.4 2.3 copy-done.2
  293.8 3.3 %collective-permute-start.7 = (bf16[512,1280]{1,0:T(8,128)(2,1)S(1)}, bf16[512,1280]{1,0:T(8,128)(2,1)S(1)}, u32[]{:S(2)}, u32[]{:S(2)}) collective-permute-start(bf16[512,1280]{1,0:T(8,128)(2,1)S(1)} %dynamic-slice_convert_fusion), channel_id=1, source_target_pairs={{0,1},{1,0},{2,3},{3,2},{4,5},{5,4},{6,7},{7,6},{8,9},{9,8},{10,11... | collective-permute-start | bytes 3932168 | tf_op jit(solution)/shard_map/ppermute | solution.py:20
  297.4 2.2 collective-permute-done.8
  301.7 3.2 %multiply_convert_fusion.1 = bf16[512,1280]{1,0:T(8,128)(2,1)} fusion(bf16[512,1280]{1,0:T(8,128)(2,1)S(1)} %collective-permute-done.7, f32[512,2560]{1,0:T(8,128)} %copy-done.2, s32[]{:T(128)S(6)} %select_n.43, f32[512]{0:T(512)S(1)} %add_rsqrt_fusion), kind=kLoop, calls=%fused_computation.12 | loop fusion | flops 2621440 | bytes 5244932 | tf_op jit(solution)/shard_map/convert_element_type | solution.py:414
  (154 shorter events, 30.0 us)
Async XLA Ops:
  6.5 8.6 %copy-start = (bf16[320,256]{1,0:T(8,128)(2,1)S(1)}, bf16[320,256]{1,0:T(8,128)(2,1)}, u32[]{:S(2)}) copy-start(bf16[320,256]{1,0:T(8,128)(2,1)} %param.15) | copy-start | bytes 491524
  6.5 221.5 %all-gather.3.cloned.1.call-start = ((), (), s32[]{:S(2)}) async-start(), calls=%async_computation | async-start | bytes 3686400 | tf_op jit(solution)/shard_map/all_gather | solution.py:292
  15.2 149.0 %copy-start.5 = (bf16[512,2560]{1,0:T(8,128)(2,1)S(1)}, bf16[512,2560]{1,0:T(8,128)(2,1)}, u32[]{:S(2)}) copy-start(bf16[512,2560]{1,0:T(8,128)(2,1)} %x_ref.1) | copy-start | bytes 7864324
  166.6 5.8 %copy-start.11 = (bf16[2,512,2560]{2,1,0:T(8,128)(2,1)}, bf16[2,512,2560]{2,1,0:T(8,128)(2,1)S(1)}, u32[]{:S(2)}) copy-start(bf16[2,512,2560]{2,1,0:T(8,128)(2,1)S(1)} %pad_maximum_fusion) | copy-start | bytes 15728644
  167.3 9.1 %copy-start.21 = (f32[1280]{0:T(1024)S(1)}, f32[1280]{0:T(1024)}, u32[]{:S(2)}) copy-start(f32[1280]{0:T(1024)} %param.18) | copy-start | bytes 15364
  167.3 9.1 %copy-start.25 = (f32[20]{0:T(128)S(1)}, f32[20]{0:T(128)}, u32[]{:S(2)}) copy-start(f32[20]{0:T(128)} %param.21) | copy-start | bytes 244
  167.3 9.2 %copy-start.26 = (f32[20]{0:T(128)S(1)}, f32[20]{0:T(128)}, u32[]{:S(2)}) copy-start(f32[20]{0:T(128)} %param.22) | copy-start | bytes 244
  167.3 12.2 %copy-start.19 = (f32[4,1280]{1,0:T(4,128)S(1)}, f32[4,1280]{1,0:T(4,128)}, u32[]{:S(2)}) copy-start(f32[4,1280]{1,0:T(4,128)} %param.17) | copy-start | bytes 61444
  167.3 12.4 %copy-start.23 = (f32[256]{0:T(256)S(1)}, f32[256]{0:T(256)}, u32[]{:S(2)}) copy-start(f32[256]{0:T(256)} %param.20) | copy-start | bytes 3076
  173.7 7.6 %collective-permute-start = (bf16[1024,128]{0,1:T(8,128)(2,1)S(1)}, bf16[1024,128]{0,1:T(8,128)(2,1)S(1)}, u32[]{:S(2)}, u32[]{:S(2)}) collective-permute-start(bf16[1024,128]{0,1:T(8,128)(2,1)S(1)} %get-tuple-element.44), channel_id=1, source_target_pairs={{0,1},{1,0},{2,3},{3,2},{4,5},{5,4},{6,7},{7,6},{8,9},{9,8},{10,11... | collective-permute-start | bytes 786440 | tf_op jit(solution)/shard_map/ppermute | solution.py:20
  185.8 6.9 %collective-permute-start.1 = (bf16[2,3,896]{2,1,0:T(4,128)(2,1)S(1)}, bf16[2,3,896]{2,1,0:T(4,128)(2,1)S(1)}, u32[]{:S(2)}, u32[]{:S(2)}) collective-permute-start(bf16[2,3,896]{2,1,0:T(4,128)(2,1)S(1)} %slice.172), channel_id=1, source_target_pairs={{0,2},{2,4},{4,6},{6,8},{8,10},{10,12},{12,14},{1,3},{3,5},{5,7},{... | collective-permute-start | bytes 32264 | tf_op jit(solution)/shard_map/ppermute | solution.py:25
  189.9 9.2 %copy-start.6 = (f32[4,256,640]{2,1,0:T(8,128)S(1)}, f32[4,256,640]{2,1,0:T(8,128)}, u32[]{:S(2)}) copy-start(f32[4,256,640]{2,1,0:T(8,128)} %copy.47) | copy-start | bytes 7864324
  189.9 10.0 %copy-start.12 = (f32[2,640]{0,1:T(8,128)}, f32[2,640]{0,1:T(8,128)S(1)}, u32[]{:S(2)}) copy-start(f32[2,640]{0,1:T(8,128)S(1)} %bitcast_multiply_fusion.1) | copy-start | bytes 15364
  199.0 7.8 %copy-start.3 = (bf16[2,512,896]{2,1,0:T(8,128)(2,1)}, bf16[2,512,896]{2,1,0:T(8,128)(2,1)S(1)}, u32[]{:S(2)}) copy-start(bf16[2,512,896]{2,1,0:T(8,128)(2,1)S(1)} %multiply_convert_fusion) | copy-start | bytes 5505028
  199.8 5.3 %copy-start.9 = (f32[2,1,640,128]{3,2,1,0:T(8,128)}, f32[2,1,640,128]{3,2,1,0:T(8,128)S(1)}, u32[]{:S(2)}) copy-start(f32[2,1,640,128]{3,2,1,0:T(8,128)S(1)} %get-tuple-element.50) | copy-start | bytes 1966084
  203.9 11.6 %collective-permute-start.2 = (bf16[2,656,128]{2,0,1:T(2,128)(2,1)}, bf16[2,656,128]{2,0,1:T(2,128)(2,1)}, u32[]{:S(2)}, u32[]{:S(2)}) collective-permute-start(bf16[2,656,128]{2,0,1:T(2,128)(2,1)} %fusion.20), channel_id=1, source_target_pairs={{0,2},{2,4},{4,6},{6,8},{8,10},{10,12},{12,14},{1,3},{3,5},{5,7},{... | collective-permute-start | bytes 1007624 | tf_op jit(solution)/shard_map/ppermute | solution.py:25
  205.2 18.4 %collective-permute-start.3 = (bf16[2,656,128]{2,0,1:T(2,128)(2,1)}, bf16[2,656,128]{2,0,1:T(2,128)(2,1)}, u32[]{:S(2)}, u32[]{:S(2)}) collective-permute-start(bf16[2,656,128]{2,0,1:T(2,128)(2,1)} %fusion.20), channel_id=1, source_target_pairs={{0,4},{2,6},{4,8},{6,10},{8,12},{10,14},{1,5},{3,7},{5,9},{7,11},{... | collective-permute-start | bytes 1007624 | tf_op jit(solution)/shard_map/ppermute | solution.py:25
  226.7 10.1 %collective-permute-start.4 = (bf16[2,656,128]{2,0,1:T(2,128)(2,1)S(1)}, bf16[2,656,128]{2,0,1:T(2,128)(2,1)}, u32[]{:S(2)}, u32[]{:S(2)}) collective-permute-start(bf16[2,656,128]{2,0,1:T(2,128)(2,1)S(1)} %pad_maximum_fusion.5), channel_id=1, source_target_pairs={{0,4},{2,6},{4,8},{6,10},{8,12},{10,14},{1,5},{3,7},{5,9},{7,11},{... | collective-permute-start | bytes 1007624 | tf_op jit(solution)/shard_map/ppermute | solution.py:25
  243.6 18.2 %collective-permute-start.5 = (bf16[2,656,128]{2,0,1:T(2,128)(2,1)}, bf16[2,656,128]{2,0,1:T(2,128)(2,1)}, u32[]{:S(2)}, u32[]{:S(2)}) collective-permute-start(bf16[2,656,128]{2,0,1:T(2,128)(2,1)} %pad_maximum_fusion.6), channel_id=1, source_target_pairs={{0,8},{2,10},{4,12},{6,14},{1,9},{3,11},{5,13},{7,15},{16,24},{18,... | collective-permute-start | bytes 1007624 | tf_op jit(solution)/shard_map/ppermute | solution.py:25
  246.8 3.3 %copy-start.27 = (f32[20]{0:T(128)S(1)}, f32[20]{0:T(128)}, u32[]{:S(2)}) copy-start(f32[20]{0:T(128)} %param.23) | copy-start | bytes 244
  246.8 3.5 %copy-start.22 = (f32[1280]{0:T(1024)S(1)}, f32[1280]{0:T(1024)}, u32[]{:S(2)}) copy-start(f32[1280]{0:T(1024)} %param.24) | copy-start | bytes 15364
  250.1 11.8 %copy-start.10 = (f32[2,1,640,128]{3,2,1,0:T(8,128)S(1)}, f32[2,1,640,128]{3,2,1,0:T(8,128)}, u32[]{:S(2)}) copy-start(f32[2,1,640,128]{3,2,1,0:T(8,128)} %copy-done.9) | copy-start | bytes 1966084
  250.5 11.4 %copy-start.13 = (f32[2,640]{0,1:T(8,128)S(1)}, f32[2,640]{0,1:T(8,128)}, u32[]{:S(2)}) copy-start(f32[2,640]{0,1:T(8,128)} %copy-done.12) | copy-start | bytes 15364
  250.5 11.4 %copy-start.15 = (f32[2,640,128]{2,0,1:T(2,128)S(1)}, f32[2,640,128]{2,0,1:T(2,128)}, u32[]{:S(2)}) copy-start(f32[2,640,128]{2,0,1:T(2,128)} %get-tuple-element.32) | copy-start | bytes 1966084
  261.9 7.3 %copy-start.4 = (bf16[2,512,896]{2,1,0:T(8,128)(2,1)S(1)}, bf16[2,512,896]{2,1,0:T(8,128)(2,1)}, u32[]{:S(2)}) copy-start(bf16[2,512,896]{2,1,0:T(8,128)(2,1)} %copy-done.3) | copy-start | bytes 5505028
  269.2 4.9 %slice-start = ((s8[6553600]{0:T(1024)(128)(4,1)}), s8[4194304]{0:T(1024)(128)(4,1)S(1)}, s32[]{:S(2)}) async-start(s8[6553600]{0:T(1024)(128)(4,1)} %bitcast.123), calls=%async_computation.1 | async-start | bytes 8388608
  270.8 3.2 %slice-start.1 = ((s8[6553600]{0:T(1024)(128)(4,1)}), s8[2359296]{0:T(1024)(128)(4,1)S(1)}, s32[]{:S(2)}) async-start(s8[6553600]{0:T(1024)(128)(4,1)} %bitcast.123), calls=%async_computation.2 | async-start | bytes 4718592
  273.8 14.2 %collective-permute-start.6 = (bf16[512,640]{1,0:T(8,128)(2,1)}, bf16[512,640]{1,0:T(8,128)(2,1)}, u32[]{:S(2)}, u32[]{:S(2)}) collective-permute-start(bf16[512,640]{1,0:T(8,128)(2,1)} %slice_bitcast_fusion), channel_id=1, source_target_pairs={{0,16},{16,0},{1,17},{17,1},{2,18},{18,2},{3,19},{19,3},{4,20},{20... | collective-permute-start | bytes 1966088 | tf_op jit(solution)/shard_map/ppermute | solution.py:20
  293.8 7.9 %collective-permute-start.7 = (bf16[512,1280]{1,0:T(8,128)(2,1)S(1)}, bf16[512,1280]{1,0:T(8,128)(2,1)S(1)}, u32[]{:S(2)}, u32[]{:S(2)}) collective-permute-start(bf16[512,1280]{1,0:T(8,128)(2,1)S(1)} %dynamic-slice_convert_fusion), channel_id=1, source_target_pairs={{0,1},{1,0},{2,3},{3,2},{4,5},{5,4},{6,7},{7,6},{8,9},{9,8},{10,11... | collective-permute-start | bytes 3932168 | tf_op jit(solution)/shard_map/ppermute | solution.py:20
  297.2 2.5 collective-permute-start.8
  299.6 2.0 collective-permute-start.9
  301.7 3.2 %copy-start.1 = (bf16[320,256]{1,0:T(8,128)(2,1)S(1)}, bf16[320,256]{1,0:T(8,128)(2,1)}, u32[]{:S(2)}) copy-start(bf16[320,256]{1,0:T(8,128)(2,1)} %param.15) | copy-start | bytes 491524
  (9 other events, 17.4 us)
Sparse Core Ops, SparseCore 0:
  13.1 96.6 all-gather.2

commit v4 on v3

--- a/solution.py
+++ b/solution.py
@@ -289,8 +289,9 @@
             for d in range(groups)
         ]
     )
-    z_all = lax.all_gather(mine(zx_weight[:, 0, :], 1, width), "seq", axis=0, tiled=True)
     first_all, out_pieces, arrived = gathered((groups, seqs, cores), first, out_t, inputs)
+    z_own, first_all = lax.optimization_barrier((mine(zx_weight[:, 0, :], 1, width), first_all))
+    z_all = lax.all_gather(z_own, "seq", axis=0, tiled=True)
     first_all = first_all.reshape(seqs * slab, first.shape[1])
     out_pieces = [out_pieces[d].reshape(-1, width) for d in range(groups)]
     batch = jnp.concatenate([inputs[None], arrived], axis=0).reshape(groups * rows, depth)
@@ -369,7 +370,7 @@
     reach = 2
     while reach < seqs - 1:
         far = shifted(packed(state, decay), "seq", reach)
-        if reach == 2:
+        if 2 * reach >= seqs - 1:
             far, gate_z = lax.optimization_barrier((far, gate_z))
         far_state, far_decay = unpacked(far)
         state = state + wide(decay)[:, :, None] * far_state

time: 312 us -> 307 us (0.984)
  Pallas kernels: 152 us -> 115 us
  waiting for transfers between devices: 35.9 us -> 66.2 us
    pallas_call x1, Pallas kernels: 148 us -> 112 us  [gathered(): pl.pallas_call(functools.partial(gather_kernel, sizes), in_specs=[anywher...]
    ppermute x5, waiting for transfers between devices: 25.6 us -> 53.7 us  [shifted(): lax.ppermute(block, axis, [(i, i + distance) for i in range(size - distan...]
  transfers between devices with their start and end apart: 11 -> 11, of which waited for: 7 -> 8; matrix products, arithmetic and copies ran while one was open for 19% -> 18% of each run, Pallas kernels for 49% -> 1%
where the time goes in v4:
time: 307 us; the launch traced here: 306 us
  Pallas kernels  115 us (37%)
  waiting for transfers between devices  66.2 us (22%)
  other arithmetic  41.7 us (14%)
  local copies, waits for them, and re-layouts  33 us (11%)
  matrix products  23.7 us (8%)
  between operations  14.1 us (5%)
  starting transfers between devices  12.6 us (4%)
    pallas_call x1, Pallas kernels, gathered(): pl.pallas_call(functools.partial(gather_kernel, sizes), in_specs=[anywher...  112 us
    ppermute x5, waiting for transfers between devices, shifted(): lax.ppermute(block, axis, [(i, i + distance) for i in range(size - distan...  53.7 us
    ppermute x5, waiting for transfers between devices, turned(): lax.ppermute(block, axis, [(i, (i + distance) % size) for i in range(size)])  12.4 us
    convert_element_type x3, other arithmetic, packed(): return jnp.concatenate([state.astype(BF16), extra], axis=1)  8.88 us
    unnamed x67, local copies, waits for them, and re-layouts  8.26 us
    dot_general x1, matrix products, shards(): gate_z = jnp.dot(batch, z_all, preferred_element_type=F32).astype(BF16)  7.82 us
    dot_general x2, matrix products, shards(): lax.dot_general(piece, out_pieces[d], (((1,), (1,)), ((), ())), preferred...  7.75 us
    another operation x2, other arithmetic, shards(): jnp.stack([held[b] + wide(passed[b])[:, :, None] * state for b in range(b...  7.35 us
  transfers between devices with their start and end apart: 11, of which 8 were waited for; matrix products, arithmetic and copies ran while one was open for 18% of the time, Pallas kernels for 1%

profile of v4, /device:TPU:29, one launch (start us, length us, event | category | flops | bytes accessed | tf_op | source)
XLA Modules:
  0.0 306.4 jit_solution(15602590294447837415)
XLA Ops:
  6.5 4.6 %fusion.53 = (bf16[320,1,1280]{2,1,0:T(2,128)(2,1)S(1)}, bf16[320,1,1280]{2,1,0:T(2,128)(2,1)S(1)}) fusion(bf16[320,2,1280]{2,1,0:T(2,128)(2,1)} %param.14), kind=kLoop, calls=%fused_computation.123 | loop fusion | bytes 3276800 | tf_op jit(solution)/shard_map/slice | solution.py:293
  11.1 2.6 constant_dynamic-slice_fusion.1
  14.0 2.0 copy.96
  17.9 111.6 %shard_map.127 = (bf16[8,320,896]{2,1,0:T(8,128)(2,1)}, bf16[2,8,320,640]{3,2,1,0:T(8,128)(2,1)}, bf16[1,512,2560]{2,1,0:T(8,128)(2,1)}) custom-call(bf16[320,896]{1,0:T(8,128)(2,1)} %fusion.13.first_ref, bf16[2,320,640]{2,1,0:T(8,128)(2,1)} %pad_maximum_fusion.3.out_ref, bf16[512,2560]{1,0:T(8,128)(2,1)} %x_ref.1), custom_call_target="tpu_custom_call" | custom-call | bytes 209715200 | tf_op jit(solution)/shard_map/pallas_call | solution.py:220
  129.5 2.4 pad_maximum_fusion
  132.6 6.9 %fusion.56 = (bf16[1024,896]{0,1:T(8,128)(2,1)S(1)}, f32[1024,896]{0,1:T(8,128)}) fusion(bf16[1024,2560]{1,0:T(8,128)(2,1)S(1)} %bitcast.124, bf16[2560,896]{1,0:T(8,128)(2,1)S(1)} %bitcast.145), kind=kOutput, calls=%fused_computation.126 | convolution fusion | flops 4698537984 | bytes 15335424 | tf_op jit(solution)/shard_map/dot_general | solution.py:299
  140.7 3.3 %collective-permute-start = (bf16[1024,128]{0,1:T(8,128)(2,1)S(1)}, bf16[1024,128]{0,1:T(8,128)(2,1)S(1)}, u32[]{:S(2)}, u32[]{:S(2)}) collective-permute-start(bf16[1024,128]{0,1:T(8,128)(2,1)S(1)} %get-tuple-element.48), channel_id=1, source_target_pairs={{0,1},{1,0},{2,3},{3,2},{4,5},{5,4},{6,7},{7,6},{8,9},{9,8},{10,11... | collective-permute-start | bytes 786440 | tf_op jit(solution)/shard_map/ppermute | solution.py:20
  145.4 2.3 reduce-window.6
  151.3 3.1 %copy.63 = bf16[1024,896]{1,0:T(8,128)(2,1)S(1)} copy(bf16[1024,896]{0,1:T(8,128)(2,1)} %pad_maximum_fusion.2) | data formatting | bytes 3670016 | tf_op jit(solution)/shard_map/reshape | solution.py:312
  154.5 1.5 collective-permute-start.1
  156.2 2.1 copy.48
  159.3 6.3 %multiply_convert_fusion = bf16[2,512,896]{2,1,0:T(8,128)(2,1)S(1)} fusion(bf16[2,512,896]{2,1,0:T(8,128)(2,1)} %bitcast.121, bf16[2,3,896]{2,1,0:T(4,128)(2,1)S(1)} %collective-permute-done.1, f32[896]{0:T(1024)S(1)} %get-tuple-element.29, f32[896]{0:T(1024)S(1)} %get-tuple-element.30, f32[896]{0:T(1024)S(1)} %get-tuple-element.28, ...), kind=kLoop, calls=%fused_computation.2 | loop fusion | flops 23855104 | bytes 3698688 | tf_op jit(solution)/shard_map/convert_element_type | solution.py:319
  166.5 2.9 fusion.11
  173.5 3.6 %shard_map.128 = f32[4,256,640]{2,1,0:T(8,128)S(1)} custom-call(bf16[4,256,640]{2,1,0:T(8,128)(2,1)S(1)} %slice.181.values_ref, bf16[4,256,128]{2,1,0:T(8,128)(2,1)S(1)} %get-tuple-element.47.keys_ref, bf16[4,256,128]{2,1,0:T(8,128)(2,1)S(1)} %get-tuple-element.46.queries_ref, f32[4,256,10]{2,1,0:T(8,128)S(1)} %copy.54.cum_ref, ...), custom_call_target="tpu_custom_call" | custom-call | flops 402653184 | bytes 3932160 | tf_op jit(solution)/shard_map/pallas_call | solution.py:53
  177.1 12.7 %collective-permute-done.2 = bf16[2,656,128]{2,0,1:T(2,128)(2,1)} collective-permute-done((bf16[2,656,128]{2,0,1:T(2,128)(2,1)}, bf16[2,656,128]{2,0,1:T(2,128)(2,1)}, u32[]{:S(2)}, u32[]{:S(2)}) %collective-permute-start.2) | collective-permute-done | bytes 335904 | tf_op jit(solution)/shard_map/ppermute | solution.py:25
  189.8 26.0 %collective-permute-done.3 = bf16[2,656,128]{2,0,1:T(2,128)(2,1)} collective-permute-done((bf16[2,656,128]{2,0,1:T(2,128)(2,1)}, bf16[2,656,128]{2,0,1:T(2,128)(2,1)}, u32[]{:S(2)}, u32[]{:S(2)}) %collective-permute-start.3) | collective-permute-done | bytes 335904 | tf_op jit(solution)/shard_map/ppermute | solution.py:25
  216.6 1.8 fusion.14
  220.2 1.7 broadcast_in_dim.45
  221.9 3.2 %copy.59 = f32[4,256,640]{2,1,0:T(8,128)} copy(f32[4,256,640]{1,2,0:T(8,128)} %bitcast.118) | data formatting | bytes 5242880 | tf_op jit(solution)/shard_map/reshape | solution.py:333
  225.4 4.1 %collective-permute-done.4 = bf16[2,656,128]{2,0,1:T(2,128)(2,1)} collective-permute-done((bf16[2,656,128]{2,0,1:T(2,128)(2,1)S(1)}, bf16[2,656,128]{2,0,1:T(2,128)(2,1)}, u32[]{:S(2)}, u32[]{:S(2)}) %collective-permute-start.4) | collective-permute-done | bytes 335904 | tf_op jit(solution)/shard_map/ppermute | solution.py:25
  231.0 4.1 %fusion.47 = (bf16[2,640,128]{2,0,1:T(2,128)(2,1)S(1)}, f32[2,640,128]{2,0,1:T(2,128)}) fusion(bf16[2,656,128]{2,0,1:T(2,128)(2,1)} %collective-permute-done.4, f32[2,640]{0,1:T(8,128)S(1)} %bitcast.135, bf16[2,656,128]{2,0,1:T(2,128)(2,1)} %collective-permute-done.3, f32[2,640]{0,1:T(8,128)S(1)} %bitcast.129, bf16[2,656,128]{2,0,1:T(2,128)(2,1)} %collective-permute-done.2), kind=kLoop, calls=%fused_computation.119 | loop fusion | flops 1310720 | bytes 1976320 | tf_op jit(solution)/shard_map/convert_element_type | solution.py:352
  237.7 7.8 %convolution_convert_fusion = bf16[1024,640]{1,0:T(8,128)(2,1)S(1)} fusion(bf16[1024,2560]{1,0:T(8,128)(2,1)} %bitcast.125, bf16[2560,640]{1,0:T(8,128)(2,1)} %all-gather.2.cloned.1.call-done), kind=kOutput, calls=%fused_computation.19 | convolution fusion | flops 3356098560 | bytes 9830400 | tf_op jit(solution)/shard_map/dot_general | solution.py:361
  245.5 10.2 %collective-permute-done.5 = bf16[2,656,128]{2,0,1:T(2,128)(2,1)} collective-permute-done((bf16[2,656,128]{2,0,1:T(2,128)(2,1)}, bf16[2,656,128]{2,0,1:T(2,128)(2,1)}, u32[]{:S(2)}, u32[]{:S(2)}) %collective-permute-start.5) | collective-permute-done | bytes 335904 | tf_op jit(solution)/shard_map/ppermute | solution.py:25
  255.8 6.4 %convert_bitcast_fusion = (bf16[2,1,640,128]{3,0,2,1:T(2,128)(2,1)S(1)}, bf16[2,1,640,128]{3,0,2,1:T(2,128)(2,1)S(1)}) fusion(f32[2,640,128]{2,0,1:T(2,128)S(1)} %copy-done.15, bf16[2,656,128]{2,0,1:T(2,128)(2,1)} %collective-permute-done.5, f32[2,640]{0,1:T(8,128)S(1)} %bitcast.133, f32[2,640]{0,1:T(8,128)S(1)} %bitcast.134, ...), kind=kLoop, calls=%fused_computation.47 | loop fusion | flops 1310720 | bytes 2309120 | tf_op jit(solution)/shard_map/stack | solution.py:380
  264.0 1.5 copy-done.7
  268.8 2.3 fusion.50
  271.1 4.4 %fusion.9 = f32[512,2560]{1,0:T(8,128)S(1)} fusion(bf16[2560,640]{1,0:T(8,128)(2,1)} %bitcast.127, bf16[2,512,640]{2,1,0:T(8,128)(2,1)} %copy-done.14), kind=kOutput, calls=%fused_computation.27 | convolution fusion | flops 1677721600 | bytes 9175040 | tf_op jit(solution)/shard_map/dot_general | solution.py:401
  275.5 9.2 %collective-permute-done.6 = bf16[512,640]{1,0:T(8,128)(2,1)} collective-permute-done((bf16[512,640]{1,0:T(8,128)(2,1)}, bf16[512,640]{1,0:T(8,128)(2,1)}, u32[]{:S(2)}, u32[]{:S(2)}) %collective-permute-start.6) | collective-permute-done | bytes 655392 | tf_op jit(solution)/shard_map/ppermute | solution.py:20
  284.6 3.4 %convolution_add_fusion = f32[512,2560]{1,0:T(8,128)S(1)} fusion(f32[512,2560]{1,0:T(8,128)S(1)} %fusion.9, bf16[512,640]{1,0:T(8,128)(2,1)} %collective-permute-done.6, bf16[2560,640]{1,0:T(8,128)(2,1)S(1)} %bitcast.115), kind=kOutput, calls=%fused_computation.1 | convolution fusion | flops 1679032320 | bytes 14417920 | tf_op jit(solution)/shard_map/dot_general | solution.py:401
  288.0 2.3 copy-done.2
  291.9 2.4 collective-permute-done.8
  296.4 3.2 %multiply_convert_fusion.1 = bf16[512,1280]{1,0:T(8,128)(2,1)} fusion(bf16[512,1280]{1,0:T(8,128)(2,1)S(1)} %collective-permute-done.7, f32[512,2560]{1,0:T(8,128)} %copy-done.2, s32[]{:T(128)S(6)} %select_n.43, f32[512]{0:T(512)S(1)} %add_rsqrt_fusion), kind=kLoop, calls=%fused_computation.10 | loop fusion | flops 2621440 | bytes 5244932 | tf_op jit(solution)/shard_map/convert_element_type | solution.py:415
  (153 shorter events, 30.5 us)
Async XLA Ops:
  6.5 10.5 %copy-start = (bf16[320,256]{1,0:T(8,128)(2,1)S(1)}, bf16[320,256]{1,0:T(8,128)(2,1)}, u32[]{:S(2)}) copy-start(bf16[320,256]{1,0:T(8,128)(2,1)} %param.15) | copy-start | bytes 491524
  6.5 231.1 %all-gather.2.cloned.1.call-start = ((), (), s32[]{:S(2)}) async-start(), calls=%async_computation | async-start | bytes 3686400 | tf_op jit(solution)/shard_map/all_gather | solution.py:294
  17.0 112.5 %copy-start.5 = (bf16[512,2560]{1,0:T(8,128)(2,1)S(1)}, bf16[512,2560]{1,0:T(8,128)(2,1)}, u32[]{:S(2)}) copy-start(bf16[512,2560]{1,0:T(8,128)(2,1)} %x_ref.1) | copy-start | bytes 7864324
  131.9 7.6 %copy-start.11 = (bf16[2,512,2560]{2,1,0:T(8,128)(2,1)}, bf16[2,512,2560]{2,1,0:T(8,128)(2,1)S(1)}, u32[]{:S(2)}) copy-start(bf16[2,512,2560]{2,1,0:T(8,128)(2,1)S(1)} %pad_maximum_fusion) | copy-start | bytes 15728644
  132.6 11.5 %copy-start.21 = (f32[1280]{0:T(1024)S(1)}, f32[1280]{0:T(1024)}, u32[]{:S(2)}) copy-start(f32[1280]{0:T(1024)} %param.18) | copy-start | bytes 15364
  132.6 11.6 %copy-start.25 = (f32[20]{0:T(128)S(1)}, f32[20]{0:T(128)}, u32[]{:S(2)}) copy-start(f32[20]{0:T(128)} %param.21) | copy-start | bytes 244
  132.6 11.7 %copy-start.26 = (f32[20]{0:T(128)S(1)}, f32[20]{0:T(128)}, u32[]{:S(2)}) copy-start(f32[20]{0:T(128)} %param.22) | copy-start | bytes 244
  139.5 8.8 %copy-start.19 = (f32[4,1280]{1,0:T(4,128)S(1)}, f32[4,1280]{1,0:T(4,128)}, u32[]{:S(2)}) copy-start(f32[4,1280]{1,0:T(4,128)} %param.17) | copy-start | bytes 61444
  139.5 8.8 %copy-start.23 = (f32[256]{0:T(256)S(1)}, f32[256]{0:T(256)}, u32[]{:S(2)}) copy-start(f32[256]{0:T(256)} %param.20) | copy-start | bytes 3076
  140.7 9.1 %collective-permute-start = (bf16[1024,128]{0,1:T(8,128)(2,1)S(1)}, bf16[1024,128]{0,1:T(8,128)(2,1)S(1)}, u32[]{:S(2)}, u32[]{:S(2)}) collective-permute-start(bf16[1024,128]{0,1:T(8,128)(2,1)S(1)} %get-tuple-element.48), channel_id=1, source_target_pairs={{0,1},{1,0},{2,3},{3,2},{4,5},{5,4},{6,7},{7,6},{8,9},{9,8},{10,11... | collective-permute-start | bytes 786440 | tf_op jit(solution)/shard_map/ppermute | solution.py:20
  154.5 4.9 %collective-permute-start.1 = (bf16[2,3,896]{2,1,0:T(4,128)(2,1)S(1)}, bf16[2,3,896]{2,1,0:T(4,128)(2,1)S(1)}, u32[]{:S(2)}, u32[]{:S(2)}) collective-permute-start(bf16[2,3,896]{2,1,0:T(4,128)(2,1)S(1)} %slice.172), channel_id=1, source_target_pairs={{0,2},{2,4},{4,6},{6,8},{8,10},{10,12},{12,14},{1,3},{3,5},{5,7},{... | collective-permute-start | bytes 32264 | tf_op jit(solution)/shard_map/ppermute | solution.py:25
  158.5 7.2 %copy-start.6 = (f32[4,256,640]{2,1,0:T(8,128)S(1)}, f32[4,256,640]{2,1,0:T(8,128)}, u32[]{:S(2)}) copy-start(f32[4,256,640]{2,1,0:T(8,128)} %copy.48) | copy-start | bytes 7864324
  158.5 8.0 %copy-start.12 = (f32[2,640]{0,1:T(8,128)}, f32[2,640]{0,1:T(8,128)S(1)}, u32[]{:S(2)}) copy-start(f32[2,640]{0,1:T(8,128)S(1)} %bitcast_multiply_fusion.1) | copy-start | bytes 15364
  165.6 7.8 %copy-start.3 = (bf16[2,512,896]{2,1,0:T(8,128)(2,1)}, bf16[2,512,896]{2,1,0:T(8,128)(2,1)S(1)}, u32[]{:S(2)}) copy-start(bf16[2,512,896]{2,1,0:T(8,128)(2,1)S(1)} %multiply_convert_fusion) | copy-start | bytes 5505028
  166.5 5.3 %copy-start.9 = (f32[2,1,640,128]{3,2,1,0:T(8,128)}, f32[2,1,640,128]{3,2,1,0:T(8,128)S(1)}, u32[]{:S(2)}) copy-start(f32[2,1,640,128]{3,2,1,0:T(8,128)S(1)} %get-tuple-element.54) | copy-start | bytes 1966084
  170.5 19.3 %collective-permute-start.2 = (bf16[2,656,128]{2,0,1:T(2,128)(2,1)}, bf16[2,656,128]{2,0,1:T(2,128)(2,1)}, u32[]{:S(2)}, u32[]{:S(2)}) collective-permute-start(bf16[2,656,128]{2,0,1:T(2,128)(2,1)} %fusion.15), channel_id=1, source_target_pairs={{0,2},{2,4},{4,6},{6,8},{8,10},{10,12},{12,14},{1,3},{3,5},{5,7},{... | collective-permute-start | bytes 1007624 | tf_op jit(solution)/shard_map/ppermute | solution.py:25
  171.8 44.0 %collective-permute-start.3 = (bf16[2,656,128]{2,0,1:T(2,128)(2,1)}, bf16[2,656,128]{2,0,1:T(2,128)(2,1)}, u32[]{:S(2)}, u32[]{:S(2)}) collective-permute-start(bf16[2,656,128]{2,0,1:T(2,128)(2,1)} %fusion.15), channel_id=1, source_target_pairs={{0,4},{2,6},{4,8},{6,10},{8,12},{10,14},{1,5},{3,7},{5,9},{7,11},{... | collective-permute-start | bytes 1007624 | tf_op jit(solution)/shard_map/ppermute | solution.py:25
  218.9 10.6 %collective-permute-start.4 = (bf16[2,656,128]{2,0,1:T(2,128)(2,1)S(1)}, bf16[2,656,128]{2,0,1:T(2,128)(2,1)}, u32[]{:S(2)}, u32[]{:S(2)}) collective-permute-start(bf16[2,656,128]{2,0,1:T(2,128)(2,1)S(1)} %pad_maximum_fusion.5), channel_id=1, source_target_pairs={{0,4},{2,6},{4,8},{6,10},{8,12},{10,14},{1,5},{3,7},{5,9},{7,11},{... | collective-permute-start | bytes 1007624 | tf_op jit(solution)/shard_map/ppermute | solution.py:25
  221.9 3.2 %copy-start.27 = (f32[20]{0:T(128)S(1)}, f32[20]{0:T(128)}, u32[]{:S(2)}) copy-start(f32[20]{0:T(128)} %param.23) | copy-start | bytes 244
  221.9 3.5 %copy-start.22 = (f32[1280]{0:T(1024)S(1)}, f32[1280]{0:T(1024)}, u32[]{:S(2)}) copy-start(f32[1280]{0:T(1024)} %param.24) | copy-start | bytes 15364
  236.3 19.4 %collective-permute-start.5 = (bf16[2,656,128]{2,0,1:T(2,128)(2,1)}, bf16[2,656,128]{2,0,1:T(2,128)(2,1)}, u32[]{:S(2)}, u32[]{:S(2)}) collective-permute-start(bf16[2,656,128]{2,0,1:T(2,128)(2,1)} %pad_maximum_fusion.6), channel_id=1, source_target_pairs={{0,8},{2,10},{4,12},{6,14},{1,9},{3,11},{5,13},{7,15},{16,24},{18,... | collective-permute-start | bytes 1007624 | tf_op jit(solution)/shard_map/ppermute | solution.py:25
  237.7 18.1 %copy-start.10 = (f32[2,1,640,128]{3,2,1,0:T(8,128)S(1)}, f32[2,1,640,128]{3,2,1,0:T(8,128)}, u32[]{:S(2)}) copy-start(f32[2,1,640,128]{3,2,1,0:T(8,128)} %copy-done.9) | copy-start | bytes 1966084
  237.7 18.1 %copy-start.13 = (f32[2,640]{0,1:T(8,128)S(1)}, f32[2,640]{0,1:T(8,128)}, u32[]{:S(2)}) copy-start(f32[2,640]{0,1:T(8,128)} %copy-done.12) | copy-start | bytes 15364
  237.7 18.1 %copy-start.15 = (f32[2,640,128]{2,0,1:T(2,128)S(1)}, f32[2,640,128]{2,0,1:T(2,128)}, u32[]{:S(2)}) copy-start(f32[2,640,128]{2,0,1:T(2,128)} %get-tuple-element.36) | copy-start | bytes 1966084
  255.8 7.5 %copy-start.4 = (bf16[2,512,896]{2,1,0:T(8,128)(2,1)S(1)}, bf16[2,512,896]{2,1,0:T(8,128)(2,1)}, u32[]{:S(2)}) copy-start(bf16[2,512,896]{2,1,0:T(8,128)(2,1)} %copy-done.3) | copy-start | bytes 5505028
  263.8 5.0 %slice-start = ((s8[6553600]{0:T(1024)(128)(4,1)}), s8[4194304]{0:T(1024)(128)(4,1)S(1)}, s32[]{:S(2)}) async-start(s8[6553600]{0:T(1024)(128)(4,1)} %bitcast.122), calls=%async_computation.1 | async-start | bytes 8388608
  265.6 3.3 %slice-start.1 = ((s8[6553600]{0:T(1024)(128)(4,1)}), s8[2359296]{0:T(1024)(128)(4,1)S(1)}, s32[]{:S(2)}) async-start(s8[6553600]{0:T(1024)(128)(4,1)} %bitcast.122), calls=%async_computation.2 | async-start | bytes 4718592
  268.5 16.1 %collective-permute-start.6 = (bf16[512,640]{1,0:T(8,128)(2,1)}, bf16[512,640]{1,0:T(8,128)(2,1)}, u32[]{:S(2)}, u32[]{:S(2)}) collective-permute-start(bf16[512,640]{1,0:T(8,128)(2,1)} %slice_bitcast_fusion), channel_id=1, source_target_pairs={{0,16},{16,0},{1,17},{17,1},{2,18},{18,2},{3,19},{19,3},{4,20},{20... | collective-permute-start | bytes 1966088 | tf_op jit(solution)/shard_map/ppermute | solution.py:20
  290.5 5.9 %collective-permute-start.7 = (bf16[512,1280]{1,0:T(8,128)(2,1)S(1)}, bf16[512,1280]{1,0:T(8,128)(2,1)S(1)}, u32[]{:S(2)}, u32[]{:S(2)}) collective-permute-start(bf16[512,1280]{1,0:T(8,128)(2,1)S(1)} %dynamic-slice_convert_fusion), channel_id=1, source_target_pairs={{0,1},{1,0},{2,3},{3,2},{4,5},{5,4},{6,7},{7,6},{8,9},{9,8},{10,11... | collective-permute-start | bytes 3932168 | tf_op jit(solution)/shard_map/ppermute | solution.py:20
  291.9 2.5 collective-permute-start.8
  294.4 2.0 collective-permute-start.9
  296.4 3.2 %copy-start.1 = (bf16[320,256]{1,0:T(8,128)(2,1)S(1)}, bf16[320,256]{1,0:T(8,128)(2,1)}, u32[]{:S(2)}) copy-start(bf16[320,256]{1,0:T(8,128)(2,1)} %param.15) | copy-start | bytes 491524
  (9 other events, 18.4 us)
Sparse Core Ops, SparseCore 0:
  144.2 72.1 all-gather.1
